TPU v7x, 128 devices: a whole 4x4x4 slice. The times are simulated.
128 devices in a mesh: seq: 8 (over y_hi, z), head: 16 (over y_lo, x, core).
Axes of the slice: x: 4, y: 4 (y_hi: 2, y_lo: 2; y = y_hi * 2 + y_lo), z: 4, core: 2. Of those that a mesh axis runs over, the one named last changes fastest.
Arguments:
- passages: bfloat16 [2048, 8192], P('seq', 'head'), may hold values from -6 to 6
- w_query: bfloat16 [8192, 8192], P(None, 'head'), as said below
- w_key: bfloat16 [8192, 1024], P(None, 'head'), as said below
- w_value: bfloat16 [8192, 1024], P(None, 'head'), may hold values from -0.0625 to 0.0625
- w_out: bfloat16 [8192, 8192], P('head'), may hold values from -0.0625 to 0.0625
- dec_hidden: bfloat16 [32, 4, 8192], P('seq'), may hold values from -6 to 6
- cache_keys: bfloat16 [32, 16, 2048, 128], P('seq', 'head'), may hold values from -6 to 6
- cache_values: bfloat16 [32, 16, 2048, 128], P('seq', 'head'), may hold values from -6 to 6
- cache_lengths: int32 [32], P('seq'), may hold values from 1 to 4096, as said below
- assignment: int32 [32], P('seq'), may hold values from 0 to 3
Outputs:
- p_out: bfloat16 [2048, 8192], P(('seq', 'head'))
- dec_out: bfloat16 [32, 4, 8192], P('seq')
Inputs may be any that keep to these rules, and one draw needn't show every extreme that they name: `cache_lengths`: some request has all 4096 slots live. `w_query`: entries lie within 4 * 8192 ** -0.5 of zero. `w_key`: entries lie within 6 * 8192 ** -0.5 of zero.
All inputs are finite; a program needn't handle non-finite values.
Results may differ from a plain program's by a relative error of at most 0.023.
Values may be sent and summed in bfloat16 or wider, within the bound.
A program may use at most 128 MiB of HBM per device.

v0:
```python
import math

import jax
import jax.numpy as jnp
from jax import lax
from jax.sharding import PartitionSpec as P

D = 8192
HD = 128
PLEN = 512


def swapped(block, axis, bit):
    count = lax.axis_size(axis)
    route = []
    for low in range(count):
        high = low | 1 << bit
        if high != low and high < count:
            route += [(low, high), (high, low)]
    return lax.ppermute(block, axis, route)


def shifted(block, axis, distance):
    devices = range(lax.axis_size(axis))
    route = [(i - distance, i) for i in devices if i - distance in devices]
    return lax.ppermute(block, axis, route)


def local(
    passages,
    w_query,
    w_key,
    w_value,
    w_out,
    dec_hidden,
    cache_keys,
    cache_values,
    cache_lengths,
    assignment,
):
    half_dim = HD // 2
    heads_here = w_query.shape[1] // HD
    parity = lax.axis_index("head") % 2
    lower = parity == 0
    second = lax.axis_index("seq") % 2 == 1
    scaling = 1.0 / math.sqrt(HD)
    tok_here = passages.shape[0]
    half_len = PLEN // 2
    pairs_local = tok_here // half_len
    piece = lax.all_gather(passages, "head", axis=1, tiled=True)
    sums_query = jnp.dot(piece, w_query, preferred_element_type=jnp.float32)
    sums_key = jnp.dot(piece, w_key, preferred_element_type=jnp.float32)
    sums_value = jnp.dot(piece, w_value, preferred_element_type=jnp.float32)
    pas_query = sums_query.astype(jnp.bfloat16).reshape(pairs_local, half_len, heads_here, HD)
    pas_key = sums_key.astype(jnp.bfloat16)
    pas_value = sums_value.astype(jnp.bfloat16)
    other_key, other_value = swapped((pas_key, pas_value), "head", 0)
    full_key = jnp.where(
        lower, jnp.concatenate([pas_key, other_key], 1), jnp.concatenate([other_key, pas_key], 1)
    )
    full_value = jnp.where(
        lower,
        jnp.concatenate([pas_value, other_value], 1),
        jnp.concatenate([other_value, pas_value], 1),
    )
    prior_key, prior_value = shifted((full_key, full_value), "seq", 1)
    keys_joined = jnp.concatenate(
        [prior_key.reshape(pairs_local, half_len, HD), full_key.reshape(pairs_local, half_len, HD)],
        axis=1,
    )
    values_joined = jnp.concatenate(
        [
            prior_value.reshape(pairs_local, half_len, HD),
            full_value.reshape(pairs_local, half_len, HD),
        ],
        axis=1,
    )
    scores = (
        jnp.einsum("pthd,pkd->phtk", pas_query, keys_joined, preferred_element_type=jnp.float32)
        * scaling
    )
    query_pos = jnp.arange(half_len)[:, None]
    key_pos = jnp.arange(2 * half_len)[None, :]
    allowed = jnp.where(key_pos < half_len, second, key_pos - half_len <= query_pos)
    scores = jnp.where(allowed, scores, -1e30)
    weights = jax.nn.softmax(scores, axis=-1).astype(jnp.bfloat16)
    context = jnp.einsum(
        "phtk,pkd->pthd", weights, values_joined, preferred_element_type=jnp.float32
    )
    context = context.astype(jnp.bfloat16).reshape(tok_here, heads_here * HD)
    p_out = lax.psum_scatter(
        jnp.dot(context, w_out, preferred_element_type=jnp.float32).astype(jnp.bfloat16),
        "head",
        scatter_dimension=0,
        tiled=True,
    ).astype(jnp.float32)
    p_out = p_out.astype(jnp.bfloat16)
    req_here = dec_hidden.shape[0]
    steps = dec_hidden.shape[1]
    flat = dec_hidden.reshape(req_here * steps, D)
    dec_query = (
        jnp.dot(flat, w_query, preferred_element_type=jnp.float32)
        .astype(jnp.bfloat16)
        .reshape(req_here, steps, heads_here, HD)
    )
    dec_key = (
        jnp.dot(flat, w_key, preferred_element_type=jnp.float32)
        .astype(jnp.bfloat16)
        .reshape(req_here, steps, half_dim)
    )
    dec_value = (
        jnp.dot(flat, w_value, preferred_element_type=jnp.float32)
        .astype(jnp.bfloat16)
        .reshape(req_here, steps, half_dim)
    )
    gathered_key, gathered_value = (
        lax.all_gather(full_key, "seq", axis=0, tiled=True),
        lax.all_gather(full_value, "seq", axis=0, tiled=True),
    )
    seq_count = lax.axis_size("seq")

    def by_passage(table):
        return (
            table.reshape(seq_count // 2, 2, pairs_local, half_len, HD)
            .transpose(0, 2, 1, 3, 4)
            .reshape(-1, PLEN, HD)
        )

    table_key = by_passage(gathered_key)[assignment]
    table_value = by_passage(gathered_value)[assignment]
    cache_key_here = cache_keys.reshape(req_here, -1, HD)
    cache_value_here = cache_values.reshape(req_here, -1, HD)
    causal_new = jnp.arange(steps)[None, :] <= jnp.arange(steps)[:, None]
    partner_query = swapped(dec_query, "head", 0)
    group_query = jnp.where(
        lower,
        jnp.concatenate([dec_query, partner_query], 2),
        jnp.concatenate([partner_query, dec_query], 2),
    )
    mine_query = lax.dynamic_slice_in_dim(group_query, parity * half_dim, half_dim, 3)
    low_key = cache_key_here[:, :, :half_dim]
    high_key = cache_key_here[:, :, half_dim:]
    low_value = cache_value_here[:, :, :half_dim]
    high_value = cache_value_here[:, :, half_dim:]
    mine_key = jnp.where(lower, low_key, high_key)
    give_key = jnp.where(lower, high_key, low_key)
    mine_value = jnp.where(lower, low_value, high_value)
    give_value = jnp.where(lower, high_value, low_value)
    got_key, got_value = swapped((give_key, give_value), "head", 0)
    slots_key = jnp.where(
        lower, jnp.concatenate([mine_key, got_key], 1), jnp.concatenate([got_key, mine_key], 1)
    )
    slots_value = jnp.where(
        lower,
        jnp.concatenate([mine_value, got_value], 1),
        jnp.concatenate([got_value, mine_value], 1),
    )
    chosen_key = lax.dynamic_slice_in_dim(table_key, parity * half_dim, half_dim, 2)
    chosen_value = lax.dynamic_slice_in_dim(table_value, parity * half_dim, half_dim, 2)
    part_pass = jnp.einsum(
        "rsgd,rpd->rsgp", mine_query, chosen_key, preferred_element_type=jnp.float32
    )
    part_cache = jnp.einsum(
        "rsgd,rcd->rsgc", mine_query, slots_key, preferred_element_type=jnp.float32
    )
    part_new = jnp.einsum("rsgd,rud->rsgu", mine_query, dec_key, preferred_element_type=jnp.float32)
    other_pass, other_cache, other_new = (
        swapped(part_pass.astype(jnp.bfloat16), "head", 0).astype(part_pass.dtype),
        swapped(part_cache.astype(jnp.bfloat16), "head", 0).astype(part_cache.dtype),
        swapped(part_new.astype(jnp.bfloat16), "head", 0).astype(part_new.dtype),
    )
    joined = (
        jnp.concatenate(
            [part_pass + other_pass, part_cache + other_cache, part_new + other_new], axis=-1
        )
        * scaling
    )
    ctx_len = slots_key.shape[1]
    live_cache = jnp.arange(ctx_len)[None, :] < cache_lengths[:, None]
    live_all = jnp.concatenate(
        [
            jnp.ones((req_here, steps, PLEN), dtype=bool),
            jnp.broadcast_to(live_cache[:, None, :], (req_here, steps, ctx_len)),
            jnp.broadcast_to(causal_new[None], (req_here, steps, steps)),
        ],
        axis=-1,
    )[:, :, None, :]
    joined = jnp.where(live_all, joined, -1e30)
    dec_weights = jax.nn.softmax(joined, axis=-1).astype(jnp.bfloat16)
    values_all = jnp.concatenate([chosen_value, slots_value, dec_value], axis=1)
    dec_context = jnp.einsum(
        "rsgc,rcd->rsgd", dec_weights, values_all, preferred_element_type=jnp.float32
    ).astype(jnp.bfloat16)
    keep_part = jnp.where(lower, dec_context[:, :, :heads_here], dec_context[:, :, heads_here:])
    give_part = jnp.where(lower, dec_context[:, :, heads_here:], dec_context[:, :, :heads_here])
    got_part = swapped(give_part, "head", 0)
    own_context = jnp.where(
        lower, jnp.concatenate([keep_part, got_part], 3), jnp.concatenate([got_part, keep_part], 3)
    )
    own_context = own_context.reshape(req_here * steps, heads_here * HD)
    dec_total = lax.psum(
        jnp.dot(own_context, w_out, preferred_element_type=jnp.float32).astype(jnp.bfloat16), "head"
    )
    dec_out = dec_total.reshape(req_here, steps, D)
    return (p_out, dec_out)


def solution(mesh):
    in_specs = (
        P("seq", "head"),
        P(None, "head"),
        P(None, "head"),
        P(None, "head"),
        P("head", None),
        P("seq", None, None),
        P("seq", "head", None, None),
        P("seq", "head", None, None),
        P("seq"),
        P("seq"),
    )
    out_specs = (P(("seq", "head"), None), P("seq", None, None))
    return jax.shard_map(local, mesh=mesh, in_specs=in_specs, out_specs=out_specs, check_vma=False)
```

profile of v0, /device:TPU:1, one launch (start us, length us, event | category | flops | bytes accessed | tf_op | source)
XLA Modules:
  0.0 344.7 jit_solution(9067537142626718398)
XLA Ops:
  7.2 0.7 all-gather.2.cloned.1.call-update
  8.0 1.0 reshape.229
  9.0 4.6 %convolution_convert_fusion.6 = bf16[16,512]{1,0:T(8,128)(2,1)S(1)} fusion(bf16[16,8192]{1,0:T(8,128)(2,1)S(1)} %reshape.229, bf16[8192,512]{1,0:T(8,128)(2,1)} %param.11), kind=kOutput, calls=%fused_computation.42 | convolution fusion | flops 134225920 | bytes 8667136 | tf_op jit(solution)/shard_map/dot_general | solution.py:102
  13.6 1.5 collective-permute-start.4
  15.1 2.9 copy.37
  18.0 1.5 broadcast_select_fusion.3
  19.5 2.9 copy.41
  22.5 1.5 broadcast_select_fusion.1
  24.0 0.5 collective-permute-start.9
  24.7 0.4 convolution_convert_fusion.7
  25.1 1.6 convolution_convert_fusion.8
  26.9 0.7 pad_add_fusion
  27.8 4.7 %fusion.51 = (bf16[4,4,8,4096]{3,2,1,0:T(8,128)(2,1)}, f32[4,4,8,4096]{3,2,1,0:T(8,128)}) fusion(bf16[4,4,8,64]{3,2,1,0:T(8,128)(2,1)S(1)} %fusion.38, bf16[4,2048,64]{1,2,0:T(8,128)(2,1)} %collective-permute-done.6, bf16[4,2048,64]{1,2,0:T(8,128)(2,1)} %get-tuple-element.2, pred[]{:T(512)S(6)} %eq.9), kind=kOutput, calls=%fused_computation.95 | convolution fusion | flops 77070336 | bytes 5259265 | tf_op jit(solution)/shard_map/rsgd,rcd->rsgc/dot_general | solution.py:163
  32.5 0.2 fusion.50
  32.7 0.5 collective-permute-start.8
  33.2 0.7 copy.42
  33.9 1.2 collective-permute-done.8
  35.1 0.8 copy.38
  35.9 2.2 maximum_select_fusion.1
  38.1 2.9 convert_add_fusion
  41.0 9.6 %all-gather.2.cloned.1.call-done = bf16[256,8192]{1,0:T(8,128)(2,1)} async-done(((bf16[256,512]{1,0:T(8,128)(2,1)}), bf16[256,8192]{1,0:T(8,128)(2,1)}) %all-gather.2.cloned.1.call-update) | async-done | bytes 4194320 | tf_op jit(solution)/shard_map/all_gather | solution.py:50
  50.6 3.7 %convolution_convert_fusion.5 = bf16[256,64]{0,1:T(8,128)(2,1)S(1)} fusion(bf16[256,8192]{1,0:T(8,128)(2,1)} %all-gather.2.cloned.1.call-done, bf16[8192,64]{0,1:T(8,128)(2,1)S(1)} %copy-done), kind=kOutput, calls=%fused_computation.41 | convolution fusion | flops 268451840 | bytes 5275648 | tf_op jit(solution)/shard_map/dot_general | solution.py:53
  54.3 0.4 collective-permute-start
  54.7 1.4 convolution_convert_fusion.4
  56.1 0.3 collective-permute-start.2
  56.4 6.4 %fusion.25 = bf16[32,4,8,128]{3,2,1,0:T(8,128)(2,1)} fusion(bf16[256,8192]{1,0:T(8,128)(2,1)S(1)} %copy-done.1, bf16[8192,512]{1,0:T(8,128)(2,1)} %param.11), kind=kOutput, calls=%fused_computation.38 | convolution fusion | flops 2147614720 | bytes 12845056 | tf_op jit(solution)/shard_map/dot_general | solution.py:51
  62.8 3.8 %collective-permute-start.1 = (bf16[256,128]{0,1:T(8,128)(2,1)S(1)}, bf16[256,128]{0,1:T(8,128)(2,1)}, u32[]{:S(2)}, u32[]{:S(2)}) collective-permute-start(bf16[256,128]{0,1:T(8,128)(2,1)S(1)} %maximum_select_fusion.2), channel_id=1, source_target_pairs={{0,16},{16,32},{32,48},{48,64},{64,80},{80,96},{96,112},{1,17},{17... | collective-permute-start | bytes 196616 | tf_op jit(solution)/shard_map/ppermute | solution.py:26
  66.6 29.0 %all_gather.11 = bf16[2048,128]{0,1:T(8,128)(2,1)S(1)} all-gather(bf16[256,128]{0,1:T(8,128)(2,1)S(1)} %maximum_select_fusion.2), channel_id=1, replica_groups=mesh['seq'=8,'head'=16] {'seq'}, dimensions={0}, use_global_device_ids=true | all-gather | bytes 589824 | tf_op jit(solution)/shard_map/all_gather | solution.py:118
  95.6 0.6 copy-done.7
  96.2 1.9 collective-permute-start.3
  98.1 29.5 %all_gather.10 = bf16[2048,128]{0,1:T(8,128)(2,1)S(1)} all-gather(bf16[256,128]{0,1:T(8,128)(2,1)S(1)} %maximum_select_fusion.4), channel_id=1, replica_groups=mesh['seq'=8,'head'=16] {'seq'}, dimensions={0}, use_global_device_ids=true | all-gather | bytes 589824 | tf_op jit(solution)/shard_map/all_gather | solution.py:117
  127.6 0.3 copy.51
  127.9 0.7 gather_fusion.1
  129.0 0.3 copy.50
  129.2 0.7 gather_fusion
  129.9 0.4 fusion.52
  130.2 12.5 %collective-permute-start.5 = (bf16[4,4,8,512]{3,2,1,0:T(8,128)(2,1)S(1)}, bf16[4,4,8,512]{3,2,1,0:T(8,128)(2,1)S(1)}, u32[]{:S(2)}, u32[]{:S(2)}) collective-permute-start(bf16[4,4,8,512]{3,2,1,0:T(8,128)(2,1)S(1)} %get-tuple-element.14), channel_id=1, source_target_pairs={{0,1},{1,0},{2,3},{3,2},{4,5},{5,4},{6,7},{7,6},{8,9},{9,8},{10,11... | collective-permute-start | bytes 393224 | tf_op jit(solution)/shard_map/ppermute | solution.py:20
  142.8 1.6 fusion.49
  144.4 0.3 fusion.18
  144.8 4.0 %fusion.53 = (f32[4,4,8]{2,1,0:T(4,128)S(1)}, f32[4,4,8,4612]{3,2,1,0:T(8,128)S(1)}) fusion(f32[4,4,8,4]{3,2,1,0:T(8,128)S(1)} %copy-done.10, f32[4,4,8,4096]{3,2,1,0:T(8,128)S(1)} %copy-done.5, f32[4,4,8,512]{3,2,1,0:T(8,128)S(1)} %convert_add_fusion.1, pred[4,4,4612]{2,1,0:T(4,128)(4,1)S(1)} %copy-done.9), kind=kOutput, calls=%fused_computation.97 | output fusion | flops 3546627 | bytes 4796992 | tf_op jit(solution)/shard_map/sub | solution.py:189
  148.9 0.8 fusion.26
  149.8 1.7 convolution_convert_fusion.2
  151.6 1.2 convolution_convert_fusion.1
  152.9 0.8 reshape.235
  153.7 7.7 %convolution_convert_fusion = bf16[256,8192]{1,0:T(8,128)(2,1)} fusion(bf16[256,512]{0,1:T(8,128)(2,1)S(1)} %bitcast.103, bf16[512,8192]{1,0:T(8,128)(2,1)} %param.14), kind=kOutput, calls=%fused_computation.3 | convolution fusion | flops 2149580800 | bytes 12845056 | tf_op jit(solution)/shard_map/dot_general | solution.py:92
  161.5 107.8 %all-reduce.2.cloned.1.call-done = bf16[4,4,8192]{2,1,0:T(4,128)(2,1)} async-done(((bf16[4,4,8192]{2,1,0:T(4,128)(2,1)}), bf16[4,4,8192]{2,1,0:T(4,128)(2,1)}) %all-reduce.2.cloned.1.call-update) | async-done | bytes 262160 | tf_op jit(solution)/shard_map/psum | solution.py:201
  269.3 67.1 %reduce-scatter.2.cloned.1.call-done = bf16[16,8192]{1,0:T(8,128)(2,1)} async-done(((bf16[256,8192]{1,0:T(8,128)(2,1)}), bf16[16,8192]{1,0:T(8,128)(2,1)}) %reduce-scatter.2.cloned.1.call-update) | async-done | bytes 262160 | tf_op jit(solution)/shard_map/reduce_scatter | solution.py:91
  336.4 1.7 copy.67
  (72 shorter events, 1.6 us)
Async XLA Ops:
  7.2 17.5 %copy-start = (bf16[8192,64]{0,1:T(8,128)(2,1)S(1)}, bf16[8192,64]{0,1:T(8,128)(2,1)}, u32[]{:S(2)}) copy-start(bf16[8192,64]{0,1:T(8,128)(2,1)} %param.13) | copy-start | bytes 3145732
  7.2 43.4 %all-gather.2.cloned.1.call-start = ((), (), s32[]{:S(2)}) async-start(), calls=%async_computation.1 | async-start | bytes 4456448 | tf_op jit(solution)/shard_map/all_gather | solution.py:50
  7.9 261.4 %all-reduce.2.cloned.1.call-start = ((), (), s32[]{:S(2)}) async-start(), calls=%async_computation.3 | async-start | bytes 524288 | tf_op jit(solution)/shard_map/psum | solution.py:201
  13.6 14.1 %collective-permute-start.4 = (bf16[4,4,4,128]{3,2,1,0:T(4,128)(2,1)S(1)}, bf16[4,4,4,128]{3,2,1,0:T(4,128)(2,1)S(1)}, u32[]{:S(2)}, u32[]{:S(2)}) collective-permute-start(bf16[4,4,4,128]{3,2,1,0:T(4,128)(2,1)S(1)} %reshape.230), channel_id=1, source_target_pairs={{0,1},{1,0},{2,3},{3,2},{4,5},{5,4},{6,7},{7,6},{8,9},{9,8},{10,11... | collective-permute-start | bytes 49160 | tf_op jit(solution)/shard_map/ppermute | solution.py:20
  19.5 8.3 %collective-permute-start.6 = (bf16[4,2048,64]{1,2,0:T(8,128)(2,1)}, bf16[4,2048,64]{1,2,0:T(8,128)(2,1)}, u32[]{:S(2)}, u32[]{:S(2)}) collective-permute-start(bf16[4,2048,64]{1,2,0:T(8,128)(2,1)} %get-tuple-element.3), channel_id=1, source_target_pairs={{0,1},{1,0},{2,3},{3,2},{4,5},{5,4},{6,7},{7,6},{8,9},{9,8},{10,11... | collective-permute-start | bytes 3145736 | tf_op jit(solution)/shard_map/ppermute | solution.py:20
  24.0 2.7 copy-start.12
  24.0 3.7 %copy-start.13 = (s32[4]{0:T(128)S(1)}, s32[4]{0:T(128)}, u32[]{:S(2)}) copy-start(s32[4]{0:T(128)} %param.19) | copy-start | bytes 52
  24.0 12.0 %collective-permute-start.9 = (bf16[4,2048,64]{1,2,0:T(8,128)(2,1)}, bf16[4,2048,64]{1,2,0:T(8,128)(2,1)S(1)}, u32[]{:S(2)}, u32[]{:S(2)}) collective-permute-start(bf16[4,2048,64]{1,2,0:T(8,128)(2,1)} %get-tuple-element.5), channel_id=1, source_target_pairs={{0,1},{1,0},{2,3},{3,2},{4,5},{5,4},{6,7},{7,6},{8,9},{9,8},{10,11... | collective-permute-start | bytes 3145736 | tf_op jit(solution)/shard_map/ppermute | solution.py:20
  27.8 8.2 %copy-start.2 = (bf16[4,2048,64]{1,2,0:T(8,128)(2,1)S(1)}, bf16[4,2048,64]{1,2,0:T(8,128)(2,1)}, u32[]{:S(2)}) copy-start(bf16[4,2048,64]{1,2,0:T(8,128)(2,1)} %get-tuple-element.4) | copy-start | bytes 3145732
  32.4 5.7 %collective-permute-start.7 = (bf16[4,4,8,4096]{3,2,1,0:T(8,128)(2,1)}, bf16[4,4,8,4096]{3,2,1,0:T(8,128)(2,1)}, u32[]{:S(2)}, u32[]{:S(2)}) collective-permute-start(bf16[4,4,8,4096]{3,2,1,0:T(8,128)(2,1)} %get-tuple-element.12), channel_id=1, source_target_pairs={{0,1},{1,0},{2,3},{3,2},{4,5},{5,4},{6,7},{7,6},{8,9},{9,8},{10,11... | collective-permute-start | bytes 3145736 | tf_op jit(solution)/shard_map/ppermute | solution.py:20
  32.7 2.4 collective-permute-start.8
  35.9 2.2 copy-start.6
  41.0 13.7 %copy-start.3 = (bf16[8192,64]{0,1:T(8,128)(2,1)S(1)}, bf16[8192,64]{0,1:T(8,128)(2,1)}, u32[]{:S(2)}) copy-start(bf16[8192,64]{0,1:T(8,128)(2,1)} %param.12) | copy-start | bytes 3145732
  50.6 4.1 %copy-start.1 = (bf16[256,8192]{1,0:T(8,128)(2,1)S(1)}, bf16[256,8192]{1,0:T(8,128)(2,1)}, u32[]{:S(2)}) copy-start(bf16[256,8192]{1,0:T(8,128)(2,1)} %all-gather.2.cloned.1.call-done) | copy-start | bytes 12582916
  54.3 8.5 %collective-permute-start = (bf16[256,64]{0,1:T(8,128)(2,1)S(1)}, bf16[256,64]{0,1:T(8,128)(2,1)S(1)}, u32[]{:S(2)}, u32[]{:S(2)}) collective-permute-start(bf16[256,64]{0,1:T(8,128)(2,1)S(1)} %convolution_convert_fusion.5), channel_id=1, source_target_pairs={{0,1},{1,0},{2,3},{3,2},{4,5},{5,4},{6,7},{7,6},{8,9},{9,8},{10,11... | collective-permute-start | bytes 98312 | tf_op jit(solution)/shard_map/ppermute | solution.py:20
  56.1 39.5 %collective-permute-start.2 = (bf16[256,64]{0,1:T(8,128)(2,1)S(1)}, bf16[256,64]{0,1:T(8,128)(2,1)S(1)}, u32[]{:S(2)}, u32[]{:S(2)}) collective-permute-start(bf16[256,64]{0,1:T(8,128)(2,1)S(1)} %convolution_convert_fusion.4), channel_id=1, source_target_pairs={{0,1},{1,0},{2,3},{3,2},{4,5},{5,4},{6,7},{7,6},{8,9},{9,8},{10,11... | collective-permute-start | bytes 98312 | tf_op jit(solution)/shard_map/ppermute | solution.py:20
  62.8 87.0 %collective-permute-start.1 = (bf16[256,128]{0,1:T(8,128)(2,1)S(1)}, bf16[256,128]{0,1:T(8,128)(2,1)}, u32[]{:S(2)}, u32[]{:S(2)}) collective-permute-start(bf16[256,128]{0,1:T(8,128)(2,1)S(1)} %maximum_select_fusion.2), channel_id=1, source_target_pairs={{0,16},{16,32},{32,48},{48,64},{64,80},{80,96},{96,112},{1,17},{17... | collective-permute-start | bytes 196616 | tf_op jit(solution)/shard_map/ppermute | solution.py:26
  95.6 0.6 copy-start.7
  96.2 46.6 %collective-permute-start.3 = (bf16[256,128]{0,1:T(8,128)(2,1)S(1)}, bf16[256,128]{0,1:T(8,128)(2,1)}, u32[]{:S(2)}, u32[]{:S(2)}) collective-permute-start(bf16[256,128]{0,1:T(8,128)(2,1)S(1)} %maximum_select_fusion.4), channel_id=1, source_target_pairs={{0,16},{16,32},{32,48},{48,64},{64,80},{80,96},{96,112},{1,17},{17... | collective-permute-start | bytes 196616 | tf_op jit(solution)/shard_map/ppermute | solution.py:26
  128.7 14.0 %copy-start.8 = (bf16[256,64]{0,1:T(8,128)(2,1)S(1)}, bf16[256,64]{0,1:T(8,128)(2,1)}, u32[]{:S(2)}) copy-start(bf16[256,64]{0,1:T(8,128)(2,1)} %copy-done.7) | copy-start | bytes 98308
  130.2 14.5 %collective-permute-start.5 = (bf16[4,4,8,512]{3,2,1,0:T(8,128)(2,1)S(1)}, bf16[4,4,8,512]{3,2,1,0:T(8,128)(2,1)S(1)}, u32[]{:S(2)}, u32[]{:S(2)}) collective-permute-start(bf16[4,4,8,512]{3,2,1,0:T(8,128)(2,1)S(1)} %get-tuple-element.14), channel_id=1, source_target_pairs={{0,1},{1,0},{2,3},{3,2},{4,5},{5,4},{6,7},{7,6},{8,9},{9,8},{10,11... | collective-permute-start | bytes 393224 | tf_op jit(solution)/shard_map/ppermute | solution.py:20
  142.8 2.0 copy-start.5
  142.8 2.0 copy-start.9
  142.8 2.0 copy-start.10
  144.8 4.0 %copy-start.4 = (bf16[4,4096,64]{1,2,0:T(8,128)(2,1)S(1)}, bf16[4,4096,64]{1,2,0:T(8,128)(2,1)}, u32[]{:S(2)}) copy-start(bf16[4,4096,64]{1,2,0:T(8,128)(2,1)} %maximum_select_fusion.1) | copy-start | bytes 6291460
  144.8 4.0 %copy-start.11 = (bf16[4,4,64]{1,2,0:T(8,128)(2,1)S(1)}, bf16[4,4,64]{1,2,0:T(8,128)(2,1)}, u32[]{:S(2)}) copy-start(bf16[4,4,64]{1,2,0:T(8,128)(2,1)} %copy.42) | copy-start | bytes 6148
  144.8 6.8 %slice-start = ((s8[8388608]{0:T(1024)(128)(4,1)}), s8[4194304]{0:T(1024)(128)(4,1)S(1)}, s32[]{:S(2)}) async-start(s8[8388608]{0:T(1024)(128)(4,1)} %bitcast.95), calls=%async_computation.4 | async-start | bytes 8388608
  148.9 2.8 slice-start.1
  149.7 1.8 collective-permute-start.10
  153.7 182.8 %reduce-scatter.2.cloned.1.call-start = ((), (), s32[]{:S(2)}) async-start(), calls=%async_computation.2 | async-start | bytes 4456448 | tf_op jit(solution)/shard_map/reduce_scatter | solution.py:91
Sparse Core Ops, SparseCore 0:
  9.7 40.8 all-gather.1
  153.8 115.4 all-reduce.1
  272.4 63.9 reduce-scatter.1
where the time goes:
time: 348 us; the launch traced here: 345 us
  waiting for transfers between devices  186 us (53%)
  blocking collectives  58.5 us (17%)
  matrix products  36.4 us (10%)
  starting transfers between devices  21.5 us (6%)
  between operations  14.1 us (4%)
  local copies, waits for them, and re-layouts  14 us (4%)
  other arithmetic  13.7 us (4%)
    psum x1, waiting for transfers between devices, local(): lax.psum(jnp.dot(own_context, w_out, preferred_element_type=jnp.float32)....  108 us
    reduce_scatter x1, waiting for transfers between devices, local(): lax.psum_scatter(jnp.dot(context, w_out, preferred_element_type=jnp.float...  67.1 us
    all_gather x1, blocking collectives, local(): lax.all_gather(full_key, 'seq', axis=0, tiled=True)  29.5 us
    all_gather x1, blocking collectives, local(): lax.all_gather(full_value, 'seq', axis=0, tiled=True)  29 us
    ppermute x9, starting transfers between devices, swapped(): return lax.ppermute(block, axis, route)  15.8 us
    all_gather x1, waiting for transfers between devices, local(): piece = lax.all_gather(passages, 'head', axis=1, tiled=True)  9.58 us
    unnamed x36, local copies, waits for them, and re-layouts  8.46 us
    dot_general x1, matrix products, local(): jnp.dot(context, w_out, preferred_element_type=jnp.float32)  7.72 us
  transfers between devices with their start and end apart: 14, of which 4 were waited for; matrix products, arithmetic and copies ran while one was open for 16% of the time, Pallas kernels for 0%

commit v1 on v0

v1 whole, which is shorter than its diff:
```python
import functools
import math

import jax
import jax.numpy as jnp
from jax import lax
from jax.experimental import pallas as pl
from jax.experimental.pallas import tpu as pltpu
from jax.sharding import PartitionSpec as P

MESH = pl.DeviceIdType.MESH
F32 = jnp.float32
BF16 = jnp.bfloat16
HD = 128
TOK = 256
DEC = 16
NEG = -1e30
ROWS = ((0, 64), (64, 64), (128, 64), (192, 64))
HALF = ((0, 128), (128, 128))


def message_ids():
    names = []
    for p in range(4):
        names += [("xp", p), ("xm", p), ("y", p)]
    names += [("xpf", 0), ("xpf", 2), ("xmf", 1), ("xmf", 3)]
    names += [("yf", dx, p) for dx in (1, 2, 3) for p in (0, 1)]
    names += [(n, p) for n in ("xpy", "xmy") for p in (2, 3)]
    names += [("xpfy", 2), ("xmfy", 3)]
    names += [("c", dx, dy, a) for dx in range(4) for dy in range(2) for a in range(2)]
    names += [("wo", i) for i in range(4)]
    names += ["kvh", "dq", "swap"]
    names += [("ctx", i) for i in range(4)]
    names += [("m1", i) for i in range(4)] + [("m2", i) for i in range(4)] + [("m3", i) for i in range(4)]
    names += [("ry", i) for i in range(4)]
    names += [("fin", i) for i in range(4)]
    names += ["part", "dctx", "dall"]
    names += [("dr", i) for i in range(1, 8)] + [("db", i) for i in range(1, 8)]
    return {n: i for i, n in enumerate(names)}


IDS = message_ids()
COUNT = len(IDS)


def dot(a, b):
    return jnp.dot(a, b, preferred_element_type=F32)


def dot_t(a, b):
    return lax.dot_general(a, b, (((1,), (1,)), ((), ())), preferred_element_type=F32)


def kernel(
    pas, wq_any, wk_any, wv_any, wo_any, dec_any, ck_any, cv_any, len_ref, asg_ref,
    pout, dout,
    xg, wq, wk, wv, wo, dech, ck, cv,
    accq, acck, accv, qb, kvh, kvo, dqo, kv, kvprev, kvall, dkv,
    ctx, part, ray, rax, rbx, rby, fin, finr,
    pk, pko, dctx, dpart, dr, dfull,
    ssem, rsem, lsem, gs, gr,
):
    s = lax.axis_index("seq")
    h = lax.axis_index("head")
    c = lax.rem(h, 2)
    chip = lax.div(h, 2)
    x = lax.rem(chip, 4)
    yl = lax.div(chip, 4)
    scale = 1.0 / math.sqrt(HD)

    def chip_at(dx, dy):
        return lax.rem(yl + dy, 2) * 4 + lax.rem(x + dx, 4)

    def dev(dx, dy, dc=0):
        return (s, chip_at(dx, dy) * 2 + lax.rem(c + dc, 2))

    XP, XM, YN, CN = dev(1, 0), dev(3, 0), dev(0, 1), dev(0, 0, 1)
    swap_dev = (s + 1 - 2 * lax.rem(s, 2), h)
    sent = []

    def send(name, src, dst, to):
        m = IDS[name]
        cp = pltpu.make_async_remote_copy(
            src_ref=src, dst_ref=dst, send_sem=ssem.at[m], recv_sem=rsem.at[m],
            device_id=to, device_id_type=MESH,
        )
        cp.start()
        sent.append(cp)

    def recv(name, ref):
        m = IDS[name]
        pltpu.make_async_remote_copy(
            src_ref=ref, dst_ref=ref, send_sem=ssem.at[m], recv_sem=rsem.at[m],
            device_id=CN, device_id_type=MESH,
        ).wait_recv()

    other = 1 - c

    def xs(dx, dy, rows, core):
        return xg.at[
            chip_at(dx, dy), pl.ds(rows[0], rows[1]), pl.ds(pl.multiple_of(core * 512, 512), 512)
        ]

    def local(i, src, dst):
        cp = pltpu.make_async_copy(src, dst, lsem.at[i])
        cp.start()
        return cp

    l_pas = local(0, pas, xs(0, 0, (0, TOK), c))
    l_dec = local(1, dec_any, dech)
    l_wq = local(2, wq_any, wq)
    l_wk = local(3, wk_any, wk)
    l_wv = local(4, wv_any, wv)

    barrier = pltpu.get_barrier_semaphore()
    plane = [(dx, dy) for dy in range(2) for dx in range(4) if (dx, dy) != (0, 0)]
    for dx, dy in plane:
        pl.semaphore_signal(barrier, inc=1, device_id=dev(dx, dy), device_id_type=MESH)
    pl.semaphore_signal(barrier, inc=1, device_id=CN, device_id_type=MESH)
    for d in range(1, 8):
        pl.semaphore_signal(barrier, inc=1, device_id=(lax.rem(s + d, 8), h), device_id_type=MESH)
    pl.semaphore_wait(barrier, 15)

    for a, b, e in ((0, 1, 2), (1, 0, 3), (2, 3, 0), (3, 2, 1)):
        send(("xp", a), pas.at[pl.ds(*ROWS[a])], xs(0, 0, ROWS[a], c), XP)
        send(("xm", b), pas.at[pl.ds(*ROWS[b])], xs(0, 0, ROWS[b], c), XM)
        send(("y", e), pas.at[pl.ds(*ROWS[e])], xs(0, 0, ROWS[e], c), YN)
    for a in range(2):
        send(("c", 0, 0, a), pas.at[pl.ds(*HALF[a])], xs(0, 0, HALF[a], c), CN)

    def fwd(name, dx, dy, rows, to):
        ref = xs(dx, dy, rows, c)
        send(name, ref, ref, to)

    def got(name, dx, dy, rows):
        recv(name, xs(dx, dy, rows, c))

    def share(dx, dy, a):
        fwd(("c", dx, dy, a), dx, dy, HALF[a], CN)

    def shared(dx, dy):
        for a in range(2):
            recv(("c", dx, dy, a), xs(dx, dy, HALF[a], other))

    l_wo = local(5, wo_any.at[:, pl.ds(pl.multiple_of(c * 4096, 4096), 4096)], wo.at[c])
    l_ck = local(6, ck_any, ck)
    l_cv = local(7, cv_any, cv)

    def push_wo(i):
        send(
            ("wo", i),
            wo_any.at[pl.ds(i * 128, 128), pl.ds(pl.multiple_of(other * 4096, 4096), 4096)],
            wo.at[c, pl.ds(i * 128, 128), :],
            CN,
        )

    l_dec.wait()
    for j in range(8):
        rows = dech[:, :, j * 1024 : (j + 1) * 1024].astype(F32).reshape(DEC, 1024)
        xg[j, TOK:, :] = rows.astype(BF16)
    accq[...] = jnp.zeros_like(accq)
    acck[...] = jnp.zeros_like(acck)
    accv[...] = jnp.zeros_like(accv)

    def project_kv(dx, dy):
        j = chip_at(dx, dy)
        rows = pl.ds(pl.multiple_of(j * 1024, 1024), 1024)
        acck[...] += dot(xg[j], wk[rows, :])
        accv[...] += dot(xg[j], wv[rows, :])

    def project_q(dx, dy):
        j = chip_at(dx, dy)
        rows = pl.ds(pl.multiple_of(j * 1024, 1024), 1024)
        accq[...] += dot(xg[j], wq[rows, :])

    def project(dx, dy):
        shared(dx, dy)
        project_kv(dx, dy)
        project_q(dx, dy)

    got(("xp", 0), 3, 0, ROWS[0])
    fwd(("xpf", 0), 3, 0, ROWS[0], XP)
    fwd(("yf", 3, 0), 3, 0, ROWS[0], YN)
    got(("xm", 1), 1, 0, ROWS[1])
    fwd(("xmf", 1), 1, 0, ROWS[1], XM)
    fwd(("yf", 1, 1), 1, 0, ROWS[1], YN)
    for p in (2, 3):
        got(("y", p), 0, 1, ROWS[p])
        fwd(("xpy", p), 0, 1, ROWS[p], XP)
        fwd(("xmy", p), 0, 1, ROWS[p], XM)
    share(0, 1, 1)
    got(("xp", 1), 3, 0, ROWS[1])
    fwd(("yf", 3, 1), 3, 0, ROWS[1], YN)
    got(("xm", 0), 1, 0, ROWS[0])
    fwd(("yf", 1, 0), 1, 0, ROWS[0], YN)
    share(3, 0, 0)
    share(1, 0, 0)
    push_wo(0)
    l_pas.wait()
    l_wq.wait()
    l_wk.wait()
    l_wv.wait()
    project(0, 0)
    got(("xp", 2), 3, 0, ROWS[2])
    fwd(("xpf", 2), 3, 0, ROWS[2], XP)
    got(("xm", 3), 1, 0, ROWS[3])
    fwd(("xmf", 3), 1, 0, ROWS[3], XM)
    got(("xpf", 0), 2, 0, ROWS[0])
    fwd(("yf", 2, 0), 2, 0, ROWS[0], YN)
    got(("xmf", 1), 2, 0, ROWS[1])
    fwd(("yf", 2, 1), 2, 0, ROWS[1], YN)
    share(2, 0, 0)
    got(("xp", 3), 3, 0, ROWS[3])
    share(3, 0, 1)
    got(("xm", 2), 1, 0, ROWS[2])
    share(1, 0, 1)
    push_wo(1)
    project(3, 0)
    got(("y", 0), 0, 1, ROWS[0])
    got(("y", 1), 0, 1, ROWS[1])
    share(0, 1, 0)
    project(1, 0)
    push_wo(2)
    got(("xpy", 2), 3, 1, ROWS[2])
    fwd(("xpfy", 2), 3, 1, ROWS[2], XP)
    got(("xmy", 3), 1, 1, ROWS[3])
    fwd(("xmfy", 3), 1, 1, ROWS[3], XM)
    project(0, 1)
    push_wo(3)
    got(("xpf", 2), 2, 0, ROWS[2])
    got(("xmf", 3), 2, 0, ROWS[3])
    share(2, 0, 1)
    project(2, 0)
    got(("xpy", 3), 3, 1, ROWS[3])
    share(3, 1, 1)
    got(("xmy", 2), 1, 1, ROWS[2])
    share(1, 1, 1)
    got(("yf", 3, 0), 3, 1, ROWS[0])
    got(("yf", 3, 1), 3, 1, ROWS[1])
    share(3, 1, 0)
    got(("yf", 1, 0), 1, 1, ROWS[0])
    got(("yf", 1, 1), 1, 1, ROWS[1])
    share(1, 1, 0)
    project(3, 1)
    got(("xpfy", 2), 2, 1, ROWS[2])
    got(("xmfy", 3), 2, 1, ROWS[3])
    share(2, 1, 1)
    got(("yf", 2, 0), 2, 1, ROWS[0])
    got(("yf", 2, 1), 2, 1, ROWS[1])
    share(2, 1, 0)
    project(1, 1)
    shared(2, 1)
    project_kv(2, 1)
    kvh[0] = acck[...].astype(BF16)
    kvh[1] = accv[...].astype(BF16)
    send("kvh", kvh, kvo, CN)
    project_q(2, 1)
    qb[...] = accq[...].astype(BF16)
    send("dq", qb.at[pl.ds(TOK, DEC)], dqo, CN)
    recv("kvh", kvo)
    low = c == 0
    for i in range(2):
        mine = kvh[i].astype(F32)
        theirs = kvo[i].astype(F32)
        full = jnp.where(
            low,
            jnp.concatenate([mine, theirs], axis=1),
            jnp.concatenate([theirs, mine], axis=1),
        ).astype(BF16)
        kv[i] = full[:TOK]
        dkv[i] = full[TOK:]
    send("swap", kv, kvprev, swap_dev)
    mine_parity = lax.rem(s, 2) == c
    slot = lax.div(s, 2)

    def gather_copy(d):
        return pltpu.make_async_remote_copy(
            src_ref=kv, dst_ref=kvall.at[slot], send_sem=gs.at[d], recv_sem=gr.at[slot],
            device_id=(lax.rem(s + d, 8), h), device_id_type=MESH,
        )

    @pl.when(mine_parity)
    def _():
        for d in range(1, 8):
            gather_copy(d).start()
        kvall[slot] = kv[...]

    recv("swap", kvprev)
    second = lax.rem(s, 2) == 1
    row = lax.broadcasted_iota(jnp.int32, (TOK, TOK), 0)
    col = lax.broadcasted_iota(jnp.int32, (TOK, TOK), 1)
    for i in range(4):
        q = qb[0:TOK, i * HD : (i + 1) * HD]
        s1 = jnp.where(row >= col, dot_t(q, kv[0]) * scale, NEG)
        s0 = jnp.where(second, dot_t(q, kvprev[0]) * scale, NEG)
        m = jnp.maximum(jnp.max(s1, axis=1, keepdims=True), jnp.max(s0, axis=1, keepdims=True))
        e1 = jnp.exp(s1 - m)
        e0 = jnp.exp(s0 - m)
        inv = 1.0 / (jnp.sum(e1, axis=1, keepdims=True) + jnp.sum(e0, axis=1, keepdims=True))
        o = dot((e1 * inv).astype(BF16), kv[1]) + dot((e0 * inv).astype(BF16), kvprev[1])
        ctx[c, :, i * HD : (i + 1) * HD] = o.astype(BF16)
        ref = ctx.at[c, :, pl.ds(i * HD, HD)]
        send(("ctx", i), ref, ref, CN)

    l_wo.wait()
    for i in range(4):
        recv(("wo", i), wo.at[other, pl.ds(i * 128, 128), :])
    for i in range(4):
        recv(("ctx", i), ctx.at[other, :, pl.ds(i * HD, HD)])

    def along(f):
        return (XP, XM) if f == 1 else (XM, XP)

    def at_x(d):
        return lax.rem(x + d, 4)

    far = 1 - yl
    FLOW = {0: 1, 1: 3, 2: 1, 3: 3}

    def x_block(ci, d):
        if ci < 2:
            return part.at[ci, yl, at_x(d)]
        return part.at[ci, :, at_x(d)]

    def x_land(ci, k):
        return rax.at[ci, k] if ci < 2 else rbx.at[ci - 2, k]

    def x_start(ci):
        f = FLOW[ci]
        ahead, behind = along(f)
        send(("m1", ci), x_block(ci, 2), x_land(ci, 0), ahead)
        send(("m2", ci), x_block(ci, 4 - f), x_land(ci, 1), behind)

    def x_pass(ci):
        f = FLOW[ci]
        ahead, _ = along(f)
        recv(("m1", ci), x_land(ci, 0))
        block = x_block(ci, f)
        block[...] = (block[...].astype(F32) + x_land(ci, 0)[...].astype(F32)).astype(BF16)
        send(("m3", ci), block, x_land(ci, 2), ahead)

    def x_end(ci):
        recv(("m2", ci), x_land(ci, 1))
        recv(("m3", ci), x_land(ci, 2))
        return (
            x_block(ci, 0)[...].astype(F32)
            + x_land(ci, 1)[...].astype(F32)
            + x_land(ci, 2)[...].astype(F32)
        )

    for ci in (0, 2, 1, 3):
        cols = slice(ci * 1024, (ci + 1) * 1024)
        total = dot(ctx[0], wo[0, :, cols]) + dot(ctx[1], wo[1, :, cols])
        part[ci] = total.astype(BF16).reshape(2, 4, 32, 1024)
        if ci < 2:
            send(("ry", ci), part.at[ci, far], ray.at[ci], YN)
        else:
            x_start(ci)

    recv("dq", dqo)
    own_q = qb[TOK:, :]
    other_q = dqo[...]
    q_low = jnp.where(low, own_q.astype(F32), other_q.astype(F32)).astype(BF16)
    q_high = jnp.where(low, other_q.astype(F32), own_q.astype(F32)).astype(BF16)
    q_all = jnp.concatenate(
        [t[:, i * HD : (i + 1) * HD] for t in (q_low, q_high) for i in range(4)], axis=0
    )
    to = lax.broadcasted_iota(jnp.int32, (128, 128), 0)
    frm = lax.broadcasted_iota(jnp.int32, (128, 128), 1)
    source = (to // 64) * 64 + ((to % 16) // 4) * 16 + ((to % 64) // 16) * 4 + to % 4
    q_rows = dot((source == frm).astype(BF16), q_all).astype(BF16)

    l_ck.wait()
    l_cv.wait()

    def decode(r):
        q = jnp.concatenate([q_rows[r * 16 : r * 16 + 16], q_rows[64 + r * 16 : 80 + r * 16]], axis=0)
        pkv = kvall[asg_ref[r]]
        sc = dot_t(q, ck[r, 0]) * scale
        place = c * 2048 + lax.broadcasted_iota(jnp.int32, sc.shape, 1)
        sc = jnp.where(place < len_ref[r], sc, NEG)
        sp = dot_t(q, pkv[0]) * scale
        sn = dot_t(q, dkv[0]) * scale
        step = lax.broadcasted_iota(jnp.int32, sn.shape, 0) % 4
        new = lax.broadcasted_iota(jnp.int32, sn.shape, 1)
        sn = jnp.where(low & (new // 4 == r) & (new % 4 <= step), sn, NEG)
        m = jnp.maximum(
            jnp.max(sc, axis=1, keepdims=True),
            jnp.maximum(jnp.max(sp, axis=1, keepdims=True), jnp.max(sn, axis=1, keepdims=True)),
        )
        ec, ep, en = jnp.exp(sc - m), jnp.exp(sp - m), jnp.exp(sn - m)
        l = (
            jnp.sum(ec, axis=1, keepdims=True)
            + jnp.sum(ep, axis=1, keepdims=True)
            + jnp.sum(en, axis=1, keepdims=True)
        )
        o = dot(ec.astype(BF16), cv[r, 0]) + dot(ep.astype(BF16), pkv[1]) + dot(en.astype(BF16), dkv[1])
        for half in range(2):
            t = slice(half * 16, half * 16 + 16)
            pk[half, 0, r * 16 : r * 16 + 16] = o[t]
            pk[half, 1, r * 16 : r * 16 + 16] = jnp.broadcast_to(m[t], (16, HD))
            pk[half, 2, r * 16 : r * 16 + 16] = jnp.broadcast_to(l[t], (16, HD))

    x_pass(2)
    x_pass(3)
    for j in range(4):
        @pl.when(2 * j + c != s)
        def _():
            pltpu.make_async_remote_copy(
                src_ref=kv, dst_ref=kvall.at[j], send_sem=gs.at[0], recv_sem=gr.at[j],
                device_id=CN, device_id_type=MESH,
            ).wait_recv()

    decode(0)
    decode(1)
    for ci in range(2):
        recv(("ry", ci), ray.at[ci])
        part[ci, yl] = (part[ci, yl].astype(F32) + ray[ci].astype(F32)).astype(BF16)
        x_start(ci)
    decode(2)
    decode(3)
    send("part", pk.at[other], pko, CN)
    x_pass(0)
    x_pass(1)
    recv("part", pko)
    o1, m1, l1 = pk[c, 0], pk[c, 1], pk[c, 2]
    o2, m2, l2 = pko[0], pko[1], pko[2]
    mm = jnp.maximum(m1, m2)
    a1, a2 = jnp.exp(m1 - mm), jnp.exp(m2 - mm)
    dec_ctx = ((a1 * o1 + a2 * o2) / (a1 * l1 + a2 * l2)).astype(BF16)
    to = lax.broadcasted_iota(jnp.int32, (16, 64), 0)
    frm = lax.broadcasted_iota(jnp.int32, (16, 64), 1)
    for i in range(4):
        pick = ((to // 4) * 16 + i * 4 + to % 4 == frm).astype(BF16)
        dctx[c, :, i * HD : (i + 1) * HD] = dot(pick, dec_ctx).astype(BF16)
    send("dctx", dctx.at[c], dctx.at[c], CN)

    for ci in (2, 3):
        rbx[ci - 2, 1] = x_end(ci).astype(BF16)
        send(("ry", ci), rbx.at[ci - 2, 1, far], rby.at[ci - 2], YN)

    recv("dctx", dctx.at[other])
    for j in range(8):
        cols = slice(j * 512, (j + 1) * 512)
        dpart[j] = (dot(dctx[0], wo[0, :, cols]) + dot(dctx[1], wo[1, :, cols])).astype(BF16)
    for i in range(1, 8):
        dx, dy = i % 4, i // 4
        send(("dr", i), dpart.at[chip_at(dx, dy)], dr.at[i], dev(dx, dy))

    def finish(ci, total):
        fin[ci] = total.astype(BF16)
        send(
            ("fin", ci),
            fin.at[ci, pl.ds(pl.multiple_of(other * 16, 16), 16)],
            finr.at[ci],
            CN,
        )

    for ci in range(2):
        finish(ci, x_end(ci))

    total = dpart[chip].astype(F32)
    for i in range(1, 8):
        recv(("dr", i), dr.at[i])
        total = total + dr[i].astype(F32)
    dfull[c, chip] = total.astype(BF16)
    for i in range(1, 8):
        dx, dy = i % 4, i // 4
        ref = dfull.at[c, chip]
        send(("db", i), ref, ref, dev(dx, dy))

    for ci in (2, 3):
        recv(("ry", ci), rby.at[ci - 2])
        finish(ci, rbx[ci - 2, 1, yl].astype(F32) + rby[ci - 2].astype(F32))

    for i in range(1, 8):
        dx, dy = i % 4, i // 4
        recv(("db", i), dfull.at[c, chip_at(4 - dx, dy)])
    send("dall", dfull.at[c], dfull.at[c], CN)
    base = pl.multiple_of(c * 4096, 4096)
    far_base = pl.multiple_of(other * 4096, 4096)
    for ci in range(4):
        keep = fin[ci, pl.ds(pl.multiple_of(c * 16, 16), 16), :]
        pout[:, pl.ds(base + ci * 1024, 1024)] = keep
    for ci in range(4):
        recv(("fin", ci), finr.at[ci])
        pout[:, pl.ds(far_base + ci * 1024, 1024)] = finr[ci]
    recv("dall", dfull.at[other])
    for a in range(2):
        for j in range(8):
            at = a * 4096 + j * 512
            dout[:, at : at + 512] = dfull[a, j]

    for cp in sent:
        cp.wait_send()

    @pl.when(mine_parity)
    def _():
        for d in range(1, 8):
            gather_copy(d).wait_send()


def local(
    passages, w_query, w_key, w_value, w_out, dec_hidden, cache_keys, cache_values, cache_lengths, assignment
):
    any_spec = pl.BlockSpec(memory_space=pl.ANY)
    smem = pl.BlockSpec(memory_space=pltpu.SMEM)
    vmem = pl.BlockSpec(memory_space=pltpu.VMEM)
    V = pltpu.VMEM
    p_out, dec_out = pl.pallas_call(
        kernel,
        out_shape=(
            jax.ShapeDtypeStruct((16, 8192), BF16),
            jax.ShapeDtypeStruct((DEC, 8192), BF16),
        ),
        in_specs=[any_spec] * 8 + [smem] * 2,
        out_specs=(vmem, vmem),
        scratch_shapes=[
            V((8, TOK + DEC, 1024), BF16),
            V((8192, 512), BF16),
            V((8192, 64), BF16),
            V((8192, 64), BF16),
            V((2, 512, 4096), BF16),
            V((4, 4, 8192), BF16),
            V((4, 1, 2048, HD), BF16),
            V((4, 1, 2048, HD), BF16),
            V((TOK + DEC, 512), F32),
            V((TOK + DEC, 64), F32),
            V((TOK + DEC, 64), F32),
            V((TOK + DEC, 512), BF16),
            V((2, TOK + DEC, 64), BF16),
            V((2, TOK + DEC, 64), BF16),
            V((DEC, 512), BF16),
            V((2, TOK, HD), BF16),
            V((2, TOK, HD), BF16),
            V((4, 2, TOK, HD), BF16),
            V((2, DEC, HD), BF16),
            V((2, TOK, 512), BF16),
            V((4, 2, 4, 32, 1024), BF16),
            V((2, 4, 32, 1024), BF16),
            V((2, 3, 32, 1024), BF16),
            V((2, 3, 2, 32, 1024), BF16),
            V((2, 32, 1024), BF16),
            V((4, 32, 1024), BF16),
            V((4, 16, 1024), BF16),
            V((2, 3, 64, HD), F32),
            V((3, 64, HD), F32),
            V((2, DEC, 512), BF16),
            V((8, DEC, 512), BF16),
            V((8, DEC, 512), BF16),
            V((2, 8, DEC, 512), BF16),
            pltpu.SemaphoreType.DMA((COUNT,)),
            pltpu.SemaphoreType.DMA((COUNT,)),
            pltpu.SemaphoreType.DMA((8,)),
            pltpu.SemaphoreType.DMA((8,)),
            pltpu.SemaphoreType.DMA((4,)),
        ],
        compiler_params=pltpu.CompilerParams(
            collective_id=0, has_side_effects=True, vmem_limit_bytes=60 * 2**20
        ),
        name="layer",
    )(
        passages, w_query, w_key, w_value, w_out, dec_hidden, cache_keys, cache_values, cache_lengths, assignment
    )
    return p_out, dec_out.reshape(4, 4, 8192)


def solution(mesh):
    in_specs = (
        P("seq", "head"),
        P(None, "head"),
        P(None, "head"),
        P(None, "head"),
        P("head", None),
        P("seq", None, None),
        P("seq", "head", None, None),
        P("seq", "head", None, None),
        P("seq"),
        P("seq"),
    )
    out_specs = (P(("seq", "head"), None), P("seq", None, None))
    return jax.shard_map(local, mesh=mesh, in_specs=in_specs, out_specs=out_specs, check_vma=False)
```

time: 348 us -> 82.9 us (0.24)
  waiting for transfers between devices: 186 us -> 0 us
  Pallas kernels: 0 us -> 74 us
  blocking collectives: 58.5 us -> 0 us
  matrix products: 36.4 us -> 0 us
  starting transfers between devices: 21.5 us -> 0 us
  other arithmetic: 13.7 us -> 0 us
  between operations: 14.1 us -> 0.65 us
  local copies, waits for them, and re-layouts: 14 us -> 8.05 us
    psum x1 -> x0, waiting for transfers between devices: 108 us -> none  [local(): lax.psum(jnp.dot(own_context, w_out, preferred_element_type=jnp.float32)....]
    pallas_call x0 -> x1, Pallas kernels: none -> 74 us  [local(): pl.pallas_call(kernel, out_shape=(jax.ShapeDtypeStruct((16, 8192), BF16),...]
    reduce_scatter x1 -> x0, waiting for transfers between devices: 67.1 us -> none  [local(): lax.psum_scatter(jnp.dot(context, w_out, preferred_element_type=jnp.float...]
    all_gather x2 -> x0, blocking collectives: 58.5 us -> none  [the longest x1 29.5 us: local(): lax.all_gather(full_key, 'seq', axis=0, tiled=True)]
    dot_general x14 -> x0, matrix products: 36.4 us -> none  [the longest x1 7.72 us: local(): jnp.dot(context, w_out, preferred_element_type=jnp.float32)]
    ppermute x11 -> x0, starting transfers between devices: 21.4 us -> none  [the longest x9 15.8 us: swapped(): return lax.ppermute(block, axis, route)]
    all_gather x1 -> x0, waiting for transfers between devices: 9.58 us -> none  [local(): piece = lax.all_gather(passages, 'head', axis=1, tiled=True)]
    select_n x11 -> x0, other arithmetic: 5.64 us -> none  [the longest x1 2.16 us: local(): jnp.where(lower, jnp.concatenate([mine_value, got_value], 1), jnp.concate...]
  transfers between devices with their start and end apart: 14 -> 0, of which waited for: 4 -> 0; matrix products, arithmetic and copies ran while one was open for 16% -> 0% of each run, Pallas kernels for 0% -> 0%
where the time goes in v1:
time: 82.9 us; the launch traced here: 82.7 us
  Pallas kernels  74 us (89%)
  local copies, waits for them, and re-layouts  8.05 us (10%)
    pallas_call x1, Pallas kernels, local(): pl.pallas_call(kernel, out_shape=(jax.ShapeDtypeStruct((16, 8192), BF16),...  74 us
    unnamed x5, local copies, waits for them, and re-layouts  6.3 us
    reshape x1, local copies, waits for them, and re-layouts, local(): return (p_out, dec_out.reshape(4, 4, 8192))  1.76 us

profile of v1, /device:TPU:1, one launch (start us, length us, event | category | flops | bytes accessed | tf_op | source)
XLA Modules:
  0.0 82.7 jit_solution(13649137883407339072)
XLA Ops:
  0.6 0.0 copy-start
  0.6 2.9 %copy.12.wk_any = bf16[8192,64]{1,0:T(8,128)(2,1)} copy(bf16[8192,64]{0,1:T(8,128)(2,1)} %param.12) | data formatting | bytes 2097152 | tf_op args[2]
  3.5 0.0 copy-done
  3.5 1.8 %copy.13.wv_any = bf16[8192,64]{1,0:T(8,128)(2,1)} copy(bf16[8192,64]{0,1:T(8,128)(2,1)S(1)} %copy-done) | data formatting | bytes 2097152 | tf_op args[3]
  5.3 74.0 %layer.1 = (bf16[16,8192]{1,0:T(8,128)(2,1)}, bf16[16,8192]{1,0:T(8,128)(2,1)}) custom-call(bf16[256,512]{1,0:T(8,128)(2,1)} %pas.1, bf16[8192,512]{1,0:T(8,128)(2,1)} %wq_any.1, bf16[8192,64]{1,0:T(8,128)(2,1)} %copy.12.wk_any, bf16[8192,64]{1,0:T(8,128)(2,1)} %copy.13.wv_any, bf16[512,8192]{1,0:T(8,128)(2,1)} %wo_any.1, bf16[4,4,8192]{2,1,0:T(4,128)(2,1)} %dec_any.1, ...), custom_call_target="tpu_custom_call" | custom-call | tf_op jit(solution)/shard_map/layer/pallas_call | solution.py:510
  79.3 1.8 %reshape.7 = bf16[4,4,8192]{2,1,0:T(4,128)(2,1)} reshape(bf16[16,8192]{1,0:T(8,128)(2,1)} %get-tuple-element.5) | data formatting | bytes 524288 | tf_op jit(solution)/shard_map/reshape | solution.py:565
  81.0 1.7 %copy.15 = bf16[16,8192]{1,0:T(8,128)(2,1)} copy(bf16[16,8192]{1,0:T(8,128)(2,1)} %get-tuple-element.8) | data formatting | bytes 524288
Async XLA Ops:
  0.6 2.9 %copy-start = (bf16[8192,64]{0,1:T(8,128)(2,1)S(1)}, bf16[8192,64]{0,1:T(8,128)(2,1)}, u32[]{:S(2)}) copy-start(bf16[8192,64]{0,1:T(8,128)(2,1)} %param.13) | copy-start | bytes 3145732

commit v2 on v1

v2 whole, which is shorter than its diff:
```python
import functools
import math

import jax
import jax.numpy as jnp
from jax import lax
from jax.experimental import pallas as pl
from jax.experimental.pallas import tpu as pltpu
from jax.sharding import PartitionSpec as P

MESH = pl.DeviceIdType.MESH
F32 = jnp.float32
BF16 = jnp.bfloat16
HD = 128
TOK = 256
DEC = 16
NEG = -1e30
ROWS = ((0, 64), (64, 48), (112, 64), (176, 80))
HALF = ((0, 112), (112, 144))
WA, WB = 384, 640
WO_PIECES = 8


def message_ids():
    names = []
    for p in range(4):
        names += [("xp", p), ("xm", p), ("y", p)]
    names += [("xpf", 0), ("xpf", 2), ("xmf", 1), ("xmf", 3)]
    names += [("yf", dx, p) for dx in (1, 2, 3) for p in (0, 1)]
    names += [(n, p) for n in ("xpy", "xmy") for p in (2, 3)]
    names += [("xpfy", 2), ("xmfy", 3)]
    names += [("c", dx, dy, a) for dx in range(4) for dy in range(2) for a in range(2)]
    names += [("wo", i) for i in range(WO_PIECES)]
    names += ["wk", "wv", "dq", "swapk", "swapv"]
    names += [("ctx", i) for i in range(4)]
    names += [(n, i) for n in ("m1", "m2", "m3", "ry", "fin") for i in range(8)]
    names += ["part", "dctx", "dall"]
    names += [("dr", i) for i in range(1, 8)] + [("db", i) for i in range(1, 8)]
    return {n: i for i, n in enumerate(names)}


IDS = message_ids()
COUNT = len(IDS)


def dot(a, b):
    return jnp.dot(a, b, preferred_element_type=F32)


def dot_t(a, b):
    return lax.dot_general(a, b, (((1,), (1,)), ((), ())), preferred_element_type=F32)


def rowmax(a):
    return jnp.max(a, axis=1, keepdims=True)


def rowsum(a):
    return jnp.sum(a, axis=1, keepdims=True)


def kernel(
    pas, wq_any, wk_any, wv_any, wo_any, dec_any, ck_any, cv_any, len_ref, asg_ref,
    pout, dout,
    xg, xd, wq, wkv, wo, dech, ck, cv,
    accq, acckv, accdq, accdkv, qb, dqb, dqo, kv, kvprev, kvall, dkv,
    ctx, parta, partb, ray, rax, rbx, rby, fina, finb, finra, finrb,
    pc, pk, pko, dctx, dpart, dr, dfull,
    ssem, rsem, lsem, gs, gr,
):
    s = lax.axis_index("seq")
    h = lax.axis_index("head")
    c = lax.rem(h, 2)
    other = 1 - c
    chip = lax.div(h, 2)
    x = lax.rem(chip, 4)
    yl = lax.div(chip, 4)
    low = c == 0
    scale = 1.0 / math.sqrt(HD)

    def chip_at(dx, dy):
        return lax.rem(yl + dy, 2) * 4 + lax.rem(x + dx, 4)

    def dev(dx, dy, dc=0):
        return (s, chip_at(dx, dy) * 2 + lax.rem(c + dc, 2))

    XP, XM, YN, CN = dev(1, 0), dev(3, 0), dev(0, 1), dev(0, 0, 1)
    swap_dev = (s + 1 - 2 * lax.rem(s, 2), h)
    mate = lax.rem(s + 4, 8)
    sent = []

    def send(name, src, dst, to):
        m = IDS[name]
        cp = pltpu.make_async_remote_copy(
            src_ref=src, dst_ref=dst, send_sem=ssem.at[m], recv_sem=rsem.at[m],
            device_id=to, device_id_type=MESH,
        )
        cp.start()
        sent.append(cp)

    def recv(name, ref):
        m = IDS[name]
        pltpu.make_async_remote_copy(
            src_ref=ref, dst_ref=ref, send_sem=ssem.at[m], recv_sem=rsem.at[m],
            device_id=CN, device_id_type=MESH,
        ).wait_recv()

    def local(i, src, dst):
        cp = pltpu.make_async_copy(src, dst, lsem.at[i])
        cp.start()
        return cp

    def xs(dx, dy, rows, core):
        return xg.at[
            chip_at(dx, dy), pl.ds(rows[0], rows[1]), pl.ds(pl.multiple_of(core * 512, 512), 512)
        ]

    def kv_rows(i, core):
        return wkv.at[pl.ds(pl.multiple_of(i * HD + core * 64, 64), 64)]

    l_pas = local(0, pas, xs(0, 0, (0, TOK), c))
    l_dec = local(1, dec_any, dech)
    l_wk = local(3, wk_any, kv_rows(0, c))
    l_wv = local(4, wv_any, kv_rows(1, c))
    l_wq = local(2, wq_any, wq)

    barrier = pltpu.get_barrier_semaphore()
    plane = [(dx, dy) for dy in range(2) for dx in range(4) if (dx, dy) != (0, 0)]
    for dx, dy in plane:
        pl.semaphore_signal(barrier, inc=1, device_id=dev(dx, dy), device_id_type=MESH)
    pl.semaphore_signal(barrier, inc=1, device_id=CN, device_id_type=MESH)
    for d in range(1, 8):
        pl.semaphore_signal(barrier, inc=1, device_id=(lax.rem(s + d, 8), h), device_id_type=MESH)
    pl.semaphore_wait(barrier, 15)

    def own(name, p, to):
        send((name, p), pas.at[pl.ds(*ROWS[p])], xs(0, 0, ROWS[p], c), to)

    def fwd(name, dx, dy, rows, to):
        ref = xs(dx, dy, rows, c)
        send(name, ref, ref, to)

    def got(name, dx, dy, rows):
        recv(name, xs(dx, dy, rows, c))

    def share(dx, dy, a):
        fwd(("c", dx, dy, a), dx, dy, HALF[a], CN)

    def shared(dx, dy):
        for a in range(2):
            recv(("c", dx, dy, a), xs(dx, dy, HALF[a], other))

    own("xp", 0, XP)
    own("xm", 1, XM)
    own("y", 2, YN)
    own("xp", 2, XP)
    own("xm", 3, XM)
    own("y", 3, YN)
    own("xp", 1, XP)
    own("xm", 0, XM)
    own("y", 0, YN)
    own("y", 1, YN)
    for a in range(2):
        send(("c", 0, 0, a), pas.at[pl.ds(*HALF[a])], xs(0, 0, HALF[a], c), CN)
    send("wk", wk_any, kv_rows(0, c), CN)
    send("wv", wv_any, kv_rows(1, c), CN)
    l_ck = local(6, ck_any, ck)
    l_cv = local(7, cv_any, cv)
    l_wo = local(5, wo_any.at[:, pl.ds(pl.multiple_of(c * 4096, 4096), 4096)], wo.at[c])

    wo_rows = 512 // WO_PIECES

    def push_wo(i):
        send(
            ("wo", i),
            wo_any.at[pl.ds(i * wo_rows, wo_rows), pl.ds(pl.multiple_of(other * 4096, 4096), 4096)],
            wo.at[c, pl.ds(i * wo_rows, wo_rows), :],
            CN,
        )

    l_dec.wait()
    for j in range(8):
        rows = dech[:, :, j * 1024 : (j + 1) * 1024].astype(F32).reshape(DEC, 1024)
        xd[j] = rows.astype(BF16)
    accq[...] = jnp.zeros_like(accq)
    acckv[...] = jnp.zeros_like(acckv)

    def project_kv(dx, dy):
        j = chip_at(dx, dy)
        cols = pl.ds(pl.multiple_of(j * 1024, 1024), 1024)
        acckv[...] += dot_t(xg[j], wkv[:, cols])

    def project_q(dx, dy):
        j = chip_at(dx, dy)
        rows = pl.ds(pl.multiple_of(j * 1024, 1024), 1024)
        accq[...] += dot(xg[j], wq[rows, :])

    def project_new(j):
        q = dot(xd[j], wq[j * 1024 : (j + 1) * 1024, :])
        k = dot_t(xd[j], wkv[:, j * 1024 : (j + 1) * 1024])
        if j == 0:
            accdq[...] = q
            accdkv[...] = k
        else:
            accdq[...] += q
            accdkv[...] += k

    got(("xm", 1), 1, 0, ROWS[1])
    fwd(("yf", 1, 1), 1, 0, ROWS[1], YN)
    fwd(("xmf", 1), 1, 0, ROWS[1], XM)
    got(("y", 2), 0, 1, ROWS[2])
    fwd(("xpy", 2), 0, 1, ROWS[2], XP)
    got(("xp", 0), 3, 0, ROWS[0])
    fwd(("yf", 3, 0), 3, 0, ROWS[0], YN)
    fwd(("xpf", 0), 3, 0, ROWS[0], XP)
    l_wk.wait()
    l_wv.wait()
    l_wq.wait()
    l_pas.wait()
    got(("y", 3), 0, 1, ROWS[3])
    fwd(("xmy", 3), 0, 1, ROWS[3], XM)
    got(("xp", 2), 3, 0, ROWS[2])
    fwd(("xpf", 2), 3, 0, ROWS[2], XP)
    fwd(("xpy", 3), 0, 1, ROWS[3], XP)
    got(("xm", 3), 1, 0, ROWS[3])
    fwd(("xmf", 3), 1, 0, ROWS[3], XM)
    fwd(("xmy", 2), 0, 1, ROWS[2], XM)
    own("xp", 3, XP)
    own("xm", 2, XM)
    share(0, 1, 1)
    got(("xp", 1), 3, 0, ROWS[1])
    fwd(("yf", 3, 1), 3, 0, ROWS[1], YN)
    share(3, 0, 0)
    got(("xm", 0), 1, 0, ROWS[0])
    fwd(("yf", 1, 0), 1, 0, ROWS[0], YN)
    share(1, 0, 0)
    recv("wk", kv_rows(0, other))
    recv("wv", kv_rows(1, other))
    push_wo(0)
    project_new(0)
    project_new(1)
    got(("xmf", 1), 2, 0, ROWS[1])
    fwd(("yf", 2, 1), 2, 0, ROWS[1], YN)
    got(("xpy", 2), 3, 1, ROWS[2])
    fwd(("xpfy", 2), 3, 1, ROWS[2], XP)
    project_new(2)
    project_new(3)
    got(("xpf", 0), 2, 0, ROWS[0])
    fwd(("yf", 2, 0), 2, 0, ROWS[0], YN)
    share(2, 0, 0)
    push_wo(1)
    got(("xmy", 3), 1, 1, ROWS[3])
    fwd(("xmfy", 3), 1, 1, ROWS[3], XM)
    got(("y", 0), 0, 1, ROWS[0])
    got(("y", 1), 0, 1, ROWS[1])
    share(0, 1, 0)
    for j in range(4, 8):
        project_new(j)
    dqb[...] = accdq[...].astype(BF16)
    send("dq", dqb, dqo, CN)
    for i in range(2):
        dkv[i] = accdkv[:, i * HD : (i + 1) * HD].astype(BF16)
    shared(0, 0)
    project_kv(0, 0)
    project_q(0, 0)
    got(("xpf", 2), 2, 0, ROWS[2])
    got(("xmf", 3), 2, 0, ROWS[3])
    share(2, 0, 1)
    push_wo(2)
    shared(0, 1)
    project_kv(0, 1)
    project_q(0, 1)
    got(("yf", 3, 0), 3, 1, ROWS[0])
    got(("yf", 1, 1), 1, 1, ROWS[1])
    got(("yf", 3, 1), 3, 1, ROWS[1])
    got(("yf", 1, 0), 1, 1, ROWS[0])
    share(3, 1, 0)
    share(1, 1, 0)
    shared(2, 0)
    project_kv(2, 0)
    project_q(2, 0)
    got(("xpy", 3), 3, 1, ROWS[3])
    share(3, 1, 1)
    got(("xmy", 2), 1, 1, ROWS[2])
    share(1, 1, 1)
    got(("xp", 3), 3, 0, ROWS[3])
    share(3, 0, 1)
    got(("xm", 2), 1, 0, ROWS[2])
    share(1, 0, 1)
    got(("xpfy", 2), 2, 1, ROWS[2])
    got(("xmfy", 3), 2, 1, ROWS[3])
    share(2, 1, 1)
    got(("yf", 2, 1), 2, 1, ROWS[1])
    got(("yf", 2, 0), 2, 1, ROWS[0])
    share(2, 1, 0)
    for place in ((3, 1), (1, 1), (3, 0), (1, 0), (2, 1)):
        shared(*place)
        project_kv(*place)

    for i in range(2):
        kv[i] = acckv[:, i * HD : (i + 1) * HD].astype(BF16)
    send("swapk", kv.at[0], kvprev.at[0], swap_dev)
    send("swapv", kv.at[1], kvprev.at[1], swap_dev)
    for i in range(3, WO_PIECES):
        push_wo(i)
    for place in ((3, 1), (1, 1), (3, 0), (1, 0), (2, 1)):
        project_q(*place)
    qb[...] = accq[...].astype(BF16)

    mine_parity = lax.rem(s, 2) == c
    slot = lax.div(s, 2)
    mate_slot = lax.div(mate, 2)

    def gather_copy(d):
        first = lax.div(s, 4) * 4
        if d == 4:
            to = mate
        else:
            to = first + lax.rem(s + d % 4, 4)
        if d < 5:
            src, at = kv, slot
        else:
            src, at = kvall.at[mate_slot], mate_slot
        return pltpu.make_async_remote_copy(
            src_ref=src, dst_ref=kvall.at[at], send_sem=gs.at[d], recv_sem=gr.at[at],
            device_id=(to, h), device_id_type=MESH,
        )

    def gather_wait(j):
        pltpu.make_async_remote_copy(
            src_ref=kv, dst_ref=kvall.at[j], send_sem=gs.at[0], recv_sem=gr.at[j],
            device_id=CN, device_id_type=MESH,
        ).wait_recv()

    @pl.when(mine_parity)
    def _():
        gather_copy(4).start()
        for d in range(1, 4):
            gather_copy(d).start()
        kvall[slot] = kv[...]

    row = lax.broadcasted_iota(jnp.int32, (TOK, TOK), 0)
    col = lax.broadcasted_iota(jnp.int32, (TOK, TOK), 1)
    held = []
    for i in range(4):
        q = qb[:, i * HD : (i + 1) * HD]
        s1 = jnp.where(row >= col, dot_t(q, kv[0]) * scale, NEG)
        m1 = rowmax(s1)
        e1 = jnp.exp(s1 - m1)
        held.append((m1, rowsum(e1), dot(e1.astype(BF16), kv[1])))

    recv("dq", dqo)
    q_low = jnp.where(low, dqb[...].astype(F32), dqo[...].astype(F32)).astype(BF16)
    q_high = jnp.where(low, dqo[...].astype(F32), dqb[...].astype(F32)).astype(BF16)
    q_all = jnp.concatenate(
        [t[:, i * HD : (i + 1) * HD] for t in (q_low, q_high) for i in range(4)], axis=0
    )
    to = lax.broadcasted_iota(jnp.int32, (128, 128), 0)
    frm = lax.broadcasted_iota(jnp.int32, (128, 128), 1)
    source = (to // 64) * 64 + ((to % 16) // 4) * 16 + ((to % 64) // 16) * 4 + to % 4
    q_rows = dot((source == frm).astype(BF16), q_all).astype(BF16)
    l_ck.wait()
    l_cv.wait()

    def new_q(r):
        return jnp.concatenate(
            [q_rows[r * 16 : r * 16 + 16], q_rows[64 + r * 16 : 80 + r * 16]], axis=0
        )

    def decode_cache(r):
        q = new_q(r)
        sc = dot_t(q, ck[r, 0]) * scale
        place = c * 2048 + lax.broadcasted_iota(jnp.int32, sc.shape, 1)
        sc = jnp.where(place < len_ref[r], sc, NEG)
        sn = dot_t(q, dkv[0]) * scale
        step = lax.broadcasted_iota(jnp.int32, sn.shape, 0) % 4
        new = lax.broadcasted_iota(jnp.int32, sn.shape, 1)
        sn = jnp.where(low & (new // 4 == r) & (new % 4 <= step), sn, NEG)
        m = jnp.maximum(rowmax(sc), rowmax(sn))
        ec, en = jnp.exp(sc - m), jnp.exp(sn - m)
        pc[r, 0] = dot(ec.astype(BF16), cv[r, 0]) + dot(en.astype(BF16), dkv[1])
        pc[r, 1] = jnp.broadcast_to(m, (32, HD))
        pc[r, 2] = jnp.broadcast_to(rowsum(ec) + rowsum(en), (32, HD))

    def decode_passage(r):
        q = new_q(r)
        pkv = kvall[asg_ref[r]]
        sp = dot_t(q, pkv[0]) * scale
        o1, m1, l1 = pc[r, 0], pc[r, 1], pc[r, 2]
        m = jnp.maximum(m1, rowmax(sp))
        ep = jnp.exp(sp - m[:, :1])
        a1 = jnp.exp(m1 - m)
        o = a1 * o1 + dot(ep.astype(BF16), pkv[1])
        l = a1 * l1 + rowsum(ep)
        for half in range(2):
            t = slice(half * 16, half * 16 + 16)
            pk[half, 0, r * 16 : r * 16 + 16] = o[t]
            pk[half, 1, r * 16 : r * 16 + 16] = m[t]
            pk[half, 2, r * 16 : r * 16 + 16] = l[t]

    for r in range(4):
        decode_cache(r)

    second = lax.rem(s, 2) == 1
    recv("swapk", kvprev.at[0])
    recv("swapv", kvprev.at[1])
    for i in range(4):
        m1, l1, o1 = held[i]
        q = qb[:, i * HD : (i + 1) * HD]
        s0 = jnp.where(second, dot_t(q, kvprev[0]) * scale, NEG)
        m = jnp.maximum(m1, rowmax(s0))
        a1 = jnp.exp(m1 - m)
        e0 = jnp.exp(s0 - m)
        l = a1 * l1 + rowsum(e0)
        o = (a1 * o1 + dot(e0.astype(BF16), kvprev[1])) / l
        ctx[c, :, i * HD : (i + 1) * HD] = o.astype(BF16)
        ref = ctx.at[c, :, pl.ds(i * HD, HD)]
        send(("ctx", i), ref, ref, CN)

    @pl.when(mine_parity)
    def _():
        gather_wait(mate_slot)
        for d in range(5, 8):
            gather_copy(d).start()

    far = 1 - yl
    FLOW = (1, 3, 1, 3) * 2

    def width(ci):
        return WA if ci < 4 else WB

    def columns(ci):
        at = ci * WA if ci < 4 else 4 * WA + (ci - 4) * WB
        return slice(at, at + width(ci))

    def along(f):
        return (XP, XM) if f == 1 else (XM, XP)

    def x_block(ci, d):
        at = lax.rem(x + d, 4)
        if ci < 4:
            return parta.at[ci, yl, at]
        return partb.at[ci - 4, :, at]

    def x_land(ci, k):
        return rax.at[ci, k] if ci < 4 else rbx.at[ci - 4, k]

    def x_first(ci):
        send(("m1", ci), x_block(ci, 2), x_land(ci, 0), along(FLOW[ci])[0])

    def x_second(ci):
        f = FLOW[ci]
        send(("m2", ci), x_block(ci, 4 - f), x_land(ci, 1), along(f)[1])

    def x_pass(ci):
        f = FLOW[ci]
        recv(("m1", ci), x_land(ci, 0))
        block = x_block(ci, f)
        block[...] = (block[...].astype(F32) + x_land(ci, 0)[...].astype(F32)).astype(BF16)
        send(("m3", ci), block, x_land(ci, 2), along(f)[0])

    def x_end(ci):
        recv(("m2", ci), x_land(ci, 1))
        recv(("m3", ci), x_land(ci, 2))
        return (
            x_block(ci, 0)[...].astype(F32)
            + x_land(ci, 1)[...].astype(F32)
            + x_land(ci, 2)[...].astype(F32)
        )

    def y_first(ci):
        recv(("ry", ci), ray.at[ci])
        parta[ci, yl] = (parta[ci, yl].astype(F32) + ray[ci].astype(F32)).astype(BF16)
        x_first(ci)
        x_second(ci)

    def y_last(ci):
        land = rbx.at[ci - 4, 1]
        land[...] = x_end(ci).astype(BF16)
        send(("ry", ci), land.at[far], rby.at[ci - 4], YN)

    def finish(ci):
        if ci < 4:
            total, keep, theirs = x_end(ci), fina.at[ci], finra.at[ci]
        else:
            recv(("ry", ci), rby.at[ci - 4])
            total = rbx[ci - 4, 1, yl].astype(F32) + rby[ci - 4].astype(F32)
            keep, theirs = finb.at[ci - 4], finrb.at[ci - 4]
        keep[...] = total.astype(BF16)
        send(("fin", ci), keep.at[pl.ds(pl.multiple_of(other * 16, 16), 16)], theirs, CN)

    def out_own(ci):
        return dot(ctx[c], wo[c, :, columns(ci)])

    def out_rest(ci, total):
        total = (total + dot(ctx[other], wo[other, :, columns(ci)])).astype(BF16)
        if ci < 4:
            parta[ci] = total.reshape(2, 4, 32, WA)
            send(("ry", ci), parta.at[ci, far], ray.at[ci], YN)
        else:
            partb[ci - 4] = total.reshape(2, 4, 32, WB)
            x_first(ci)

    l_wo.wait()
    begun = out_own(0)
    for i in range(WO_PIECES):
        recv(("wo", i), wo.at[other, pl.ds(i * wo_rows, wo_rows), :])
    for i in range(4):
        recv(("ctx", i), ctx.at[other, :, pl.ds(i * HD, HD)])
    out_rest(0, begun)
    for ci in (4, 5):
        out_rest(ci, out_own(ci))
    x_second(4)
    x_second(5)
    for ci in (1, 6, 7):
        out_rest(ci, out_own(ci))
    x_second(6)
    x_second(7)
    for ci in (2, 3):
        out_rest(ci, out_own(ci))

    for j in range(4):
        @pl.when((2 * j + c != s) & (2 * j + c != mate))
        def _():
            gather_wait(j)

    for r in range(4):
        decode_passage(r)
    send("part", pk.at[other], pko, CN)
    x_pass(4)
    x_pass(5)
    y_first(0)
    recv("part", pko)
    o1, m1, l1 = pk[c, 0], pk[c, 1], pk[c, 2]
    o2, m2, l2 = pko[0], pko[1], pko[2]
    mm = jnp.maximum(m1, m2)
    a1, a2 = jnp.exp(m1 - mm), jnp.exp(m2 - mm)
    dec_ctx = ((a1 * o1 + a2 * o2) / (a1 * l1 + a2 * l2)).astype(BF16)
    to = lax.broadcasted_iota(jnp.int32, (16, 64), 0)
    frm = lax.broadcasted_iota(jnp.int32, (16, 64), 1)
    for i in range(4):
        pick = ((to // 4) * 16 + i * 4 + to % 4 == frm).astype(BF16)
        dctx[c, :, i * HD : (i + 1) * HD] = dot(pick, dec_ctx).astype(BF16)
    send("dctx", dctx.at[c], dctx.at[c], CN)
    y_first(1)
    x_pass(6)
    x_pass(7)
    recv("dctx", dctx.at[other])
    for j in range(8):
        cols = slice(j * 512, (j + 1) * 512)
        dpart[j] = (dot(dctx[0], wo[0, :, cols]) + dot(dctx[1], wo[1, :, cols])).astype(BF16)
    for i in range(1, 8):
        dx, dy = i % 4, i // 4
        send(("dr", i), dpart.at[chip_at(dx, dy)], dr.at[i], dev(dx, dy))
    y_first(2)
    x_pass(0)
    y_first(3)
    x_pass(1)
    y_last(4)
    y_last(5)
    total = dpart[chip].astype(F32)
    for i in range(1, 8):
        recv(("dr", i), dr.at[i])
        total = total + dr[i].astype(F32)
    dfull[c, chip] = total.astype(BF16)
    for i in range(1, 8):
        dx, dy = i % 4, i // 4
        ref = dfull.at[c, chip]
        send(("db", i), ref, ref, dev(dx, dy))
    y_last(6)
    y_last(7)
    x_pass(2)
    x_pass(3)
    finish(0)
    finish(1)
    for i in range(1, 8):
        dx, dy = i % 4, i // 4
        recv(("db", i), dfull.at[c, chip_at(4 - dx, dy)])
    send("dall", dfull.at[c], dfull.at[c], CN)
    for ci in (4, 5, 6, 7, 2, 3):
        finish(ci)

    recv("dall", dfull.at[other])
    for a in range(2):
        for j in range(8):
            at = a * 4096 + j * 512
            dout[:, :, at : at + 512] = dfull[a, j].astype(F32).reshape(4, 4, 512).astype(BF16)
    base = pl.multiple_of(c * 4096, 4096)
    far_base = pl.multiple_of(other * 4096, 4096)
    mine = pl.ds(pl.multiple_of(c * 16, 16), 16)
    for ci in (0, 1, 4, 5, 6, 7, 2, 3):
        at = columns(ci).start
        if ci < 4:
            keep, theirs = fina.at[ci], finra.at[ci]
        else:
            keep, theirs = finb.at[ci - 4], finrb.at[ci - 4]
        pout[:, pl.ds(base + at, width(ci))] = keep[mine, :]
        recv(("fin", ci), theirs)
        pout[:, pl.ds(far_base + at, width(ci))] = theirs[...]

    for cp in sent:
        cp.wait_send()

    @pl.when(mine_parity)
    def _():
        for d in range(1, 8):
            gather_copy(d).wait_send()


def hand_over(p_in, d_in, p_out, d_out):
    p_out[...] = p_in[...]
    d_out[...] = d_in[...]


def local(
    passages, w_query, w_key, w_value, w_out, dec_hidden, cache_keys, cache_values, cache_lengths, assignment
):
    any_spec = pl.BlockSpec(memory_space=pl.ANY)
    smem = pl.BlockSpec(memory_space=pltpu.SMEM)
    vmem = pl.BlockSpec(memory_space=pltpu.VMEM)
    V = pltpu.VMEM
    shapes = (jax.ShapeDtypeStruct((16, 8192), BF16), jax.ShapeDtypeStruct((4, 4, 8192), BF16))
    results = pl.pallas_call(
        kernel,
        out_shape=shapes,
        in_specs=[any_spec] * 8 + [smem] * 2,
        out_specs=(vmem, vmem),
        scratch_shapes=[
            V((8, TOK, 1024), BF16),
            V((8, DEC, 1024), BF16),
            V((8192, 512), BF16),
            V((2 * HD, 8192), BF16),
            V((2, 512, 4096), BF16),
            V((4, 4, 8192), BF16),
            V((4, 1, 2048, HD), BF16),
            V((4, 1, 2048, HD), BF16),
            V((TOK, 512), F32),
            V((TOK, 2 * HD), F32),
            V((DEC, 512), F32),
            V((DEC, 2 * HD), F32),
            V((TOK, 512), BF16),
            V((DEC, 512), BF16),
            V((DEC, 512), BF16),
            V((2, TOK, HD), BF16),
            V((2, TOK, HD), BF16),
            V((4, 2, TOK, HD), BF16),
            V((2, DEC, HD), BF16),
            V((2, TOK, 512), BF16),
            V((4, 2, 4, 32, WA), BF16),
            V((4, 2, 4, 32, WB), BF16),
            V((4, 4, 32, WA), BF16),
            V((4, 3, 32, WA), BF16),
            V((4, 3, 2, 32, WB), BF16),
            V((4, 32, WB), BF16),
            V((4, 32, WA), BF16),
            V((4, 32, WB), BF16),
            V((4, 16, WA), BF16),
            V((4, 16, WB), BF16),
            V((4, 3, 32, HD), F32),
            V((2, 3, 64, HD), F32),
            V((3, 64, HD), F32),
            V((2, DEC, 512), BF16),
            V((8, DEC, 512), BF16),
            V((8, DEC, 512), BF16),
            V((2, 8, DEC, 512), BF16),
            pltpu.SemaphoreType.DMA((COUNT,)),
            pltpu.SemaphoreType.DMA((COUNT,)),
            pltpu.SemaphoreType.DMA((8,)),
            pltpu.SemaphoreType.DMA((8,)),
            pltpu.SemaphoreType.DMA((4,)),
        ],
        compiler_params=pltpu.CompilerParams(
            collective_id=0, has_side_effects=True, vmem_limit_bytes=60 * 2**20
        ),
        name="layer",
    )(
        passages, w_query, w_key.T, w_value.T, w_out, dec_hidden, cache_keys, cache_values, cache_lengths, assignment
    )
    return pl.pallas_call(
        hand_over,
        out_shape=shapes,
        in_specs=[vmem] * 2,
        out_specs=(vmem, vmem),
        name="hand_over",
    )(*results)


def solution(mesh):
    in_specs = (
        P("seq", "head"),
        P(None, "head"),
        P(None, "head"),
        P(None, "head"),
        P("head", None),
        P("seq", None, None),
        P("seq", "head", None, None),
        P("seq", "head", None, None),
        P("seq"),
        P("seq"),
    )
    out_specs = (P(("seq", "head"), None), P("seq", None, None))
    return jax.shard_map(local, mesh=mesh, in_specs=in_specs, out_specs=out_specs, check_vma=False)
```

time: 82.9 us -> 67.9 us (0.82)
  local copies, waits for them, and re-layouts: 8.05 us -> 0 us
  Pallas kernels: 74 us -> 67.1 us
    pallas_call x1 -> x2, Pallas kernels: 74 us -> 67.1 us  [the longest x1 65.2 us: local(): pl.pallas_call(kernel, out_shape=shapes, in_specs=[any_spec] * 8 + [smem]...]
    unnamed x5 -> x0, local copies, waits for them, and re-layouts: 6.3 us -> none
    reshape x1 -> x0, local copies, waits for them, and re-layouts: 1.76 us -> none  [local(): return (p_out, dec_out.reshape(4, 4, 8192))]
where the time goes in v2:
time: 67.9 us; the launch traced here: 67.7 us
  Pallas kernels  67.1 us (99%)
    pallas_call x1, Pallas kernels, local(): pl.pallas_call(kernel, out_shape=shapes, in_specs=[any_spec] * 8 + [smem]...  65.2 us
    pallas_call x1, Pallas kernels, local(): pl.pallas_call(hand_over, out_shape=shapes, in_specs=[vmem] * 2, out_spec...  1.84 us

profile of v2, /device:TPU:1, one launch (start us, length us, event | category | flops | bytes accessed | tf_op | source)
XLA Modules:
  0.0 67.7 jit_solution(17327341740301701425)
XLA Ops:
  0.6 65.2 %layer.1 = (bf16[16,8192]{1,0:T(8,128)(2,1)}, bf16[4,4,8192]{2,1,0:T(4,128)(2,1)}) custom-call(bf16[256,512]{1,0:T(8,128)(2,1)} %pas.1, bf16[8192,512]{1,0:T(8,128)(2,1)} %wq_any.1, bf16[64,8192]{1,0:T(8,128)(2,1)} %bitcast.2, bf16[64,8192]{1,0:T(8,128)(2,1)} %bitcast.3, bf16[512,8192]{1,0:T(8,128)(2,1)} %wo_any.1, bf16[4,4,8192]{2,1,0:T(4,128)(2,1)} %dec_any.1, ...), custom_call_target="tpu_custom_call" | custom-call | tf_op jit(solution)/shard_map/layer/pallas_call | solution.py:623
  65.9 1.8 %hand_over.1 = (bf16[16,8192]{1,0:T(8,128)(2,1)}, bf16[4,4,8192]{2,1,0:T(4,128)(2,1)}) custom-call(bf16[16,8192]{1,0:T(8,128)(2,1)} %get-tuple-element.4.p_in, bf16[4,4,8192]{2,1,0:T(4,128)(2,1)} %get-tuple-element.5.d_in), custom_call_target="tpu_custom_call" | custom-call | tf_op jit(solution)/shard_map/hand_over/pallas_call | solution.py:679

commit v3 on v2

--- a/solution.py
+++ b/solution.py
@@ -17,7 +17,7 @@
 NEG = -1e30
 ROWS = ((0, 64), (64, 48), (112, 64), (176, 80))
 HALF = ((0, 112), (112, 144))
-WA, WB = 384, 640
+WA, WB = 512, 512
 WO_PIECES = 8
 
 
@@ -33,8 +33,11 @@
     names += [("wo", i) for i in range(WO_PIECES)]
     names += ["wk", "wv", "dq", "swapk", "swapv"]
     names += [("ctx", i) for i in range(4)]
-    names += [(n, i) for n in ("m1", "m2", "m3", "ry", "fin") for i in range(8)]
-    names += ["part", "dctx", "dall"]
+    names += [(n, i) for n in ("m1", "m2", "m3", "bl") for i in range(4, 8)]
+    names += [("ry", i) for i in range(4)]
+    names += [("ax", i, dx, q) for i in range(4) for dx in range(4) for q in range(2) if dx or q]
+    names += [("by", i, q) for i in range(4, 8) for q in range(2)]
+    names += ["part", "dall"]
     names += [("dr", i) for i in range(1, 8)] + [("db", i) for i in range(1, 8)]
     return {n: i for i, n in enumerate(names)}
 
@@ -64,8 +67,8 @@
     pout, dout,
     xg, xd, wq, wkv, wo, dech, ck, cv,
     accq, acckv, accdq, accdkv, qb, dqb, dqo, kv, kvprev, kvall, dkv,
-    ctx, parta, partb, ray, rax, rbx, rby, fina, finb, finra, finrb,
-    pc, pk, pko, dctx, dpart, dr, dfull,
+    ctx, parta, partb, ray, rax, rbx, rby, rbl,
+    pc, pk, pko, qrows, dctx, dpart, dr, dfull,
     ssem, rsem, lsem, gs, gr,
 ):
     s = lax.axis_index("seq")
@@ -125,13 +128,13 @@
     l_wq = local(2, wq_any, wq)
 
     barrier = pltpu.get_barrier_semaphore()
-    plane = [(dx, dy) for dy in range(2) for dx in range(4) if (dx, dy) != (0, 0)]
-    for dx, dy in plane:
-        pl.semaphore_signal(barrier, inc=1, device_id=dev(dx, dy), device_id_type=MESH)
-    pl.semaphore_signal(barrier, inc=1, device_id=CN, device_id_type=MESH)
-    for d in range(1, 8):
-        pl.semaphore_signal(barrier, inc=1, device_id=(lax.rem(s + d, 8), h), device_id_type=MESH)
-    pl.semaphore_wait(barrier, 15)
+    for to in (XP, XM, YN, CN):
+        pl.semaphore_signal(barrier, inc=1, device_id=to, device_id_type=MESH)
+    z_first = lax.div(s, 4) * 4
+    along_z = [z_first + lax.rem(s + d, 4) for d in range(4)]
+    for to in along_z[1:] + [mate]:
+        pl.semaphore_signal(barrier, inc=1, device_id=(to, h), device_id_type=MESH)
+    pl.semaphore_wait(barrier, 8)
 
     def own(name, p, to):
         send((name, p), pas.at[pl.ds(*ROWS[p])], xs(0, 0, ROWS[p], c), to)
@@ -195,15 +198,71 @@
         rows = pl.ds(pl.multiple_of(j * 1024, 1024), 1024)
         accq[...] += dot(xg[j], wq[rows, :])
 
-    def project_new(j):
+    def project(dx, dy):
+        shared(dx, dy)
+        project_kv(dx, dy)
+        project_q(dx, dy)
+
+    def project_new_q(j):
         q = dot(xd[j], wq[j * 1024 : (j + 1) * 1024, :])
+        accdq[...] = q if j == 0 else accdq[...] + q
+
+    def project_new_kv(j):
         k = dot_t(xd[j], wkv[:, j * 1024 : (j + 1) * 1024])
-        if j == 0:
-            accdq[...] = q
-            accdkv[...] = k
-        else:
-            accdq[...] += q
-            accdkv[...] += k
+        accdkv[...] = k if j == 0 else accdkv[...] + k
+
+    lane = lax.broadcasted_iota(jnp.int32, (16, HD), 1)
+
+    def arrange_new():
+        recv("dq", dqo)
+        q_low = jnp.where(low, dqb[...].astype(F32), dqo[...].astype(F32)).astype(BF16)
+        q_high = jnp.where(low, dqo[...].astype(F32), dqb[...].astype(F32)).astype(BF16)
+        q_all = jnp.concatenate(
+            [t[:, i * HD : (i + 1) * HD] for t in (q_low, q_high) for i in range(4)], axis=0
+        )
+        to = lax.broadcasted_iota(jnp.int32, (128, 128), 0)
+        frm = lax.broadcasted_iota(jnp.int32, (128, 128), 1)
+        source = (to // 64) * 64 + ((to % 16) // 4) * 16 + ((to % 64) // 16) * 4 + to % 4
+        qrows[...] = dot((source == frm).astype(BF16), q_all).astype(BF16)
+        l_ck.wait()
+        l_cv.wait()
+
+    def new_q(r):
+        q_rows = qrows[...]
+        return jnp.concatenate(
+            [q_rows[r * 16 : r * 16 + 16], q_rows[64 + r * 16 : 80 + r * 16]], axis=0
+        )
+
+    def decode_cache(r):
+        q = new_q(r)
+        sc = dot_t(q, ck[r, 0]) * scale
+        place = c * 2048 + lax.broadcasted_iota(jnp.int32, sc.shape, 1)
+        sc = jnp.where(place < len_ref[r], sc, NEG)
+        m = rowmax(sc)
+        ec = jnp.exp(sc - m)
+        pc[r, 0] = dot(ec.astype(BF16), cv[r, 0])
+        pc[r, 1] = jnp.broadcast_to(m, (32, HD))
+        pc[r, 2] = jnp.broadcast_to(rowsum(ec), (32, HD))
+
+    def decode_passage(r):
+        q = new_q(r)
+        pkv = kvall[asg_ref[r]]
+        sp = dot_t(q, pkv[0]) * scale
+        sn = dot_t(q, dkv[0]) * scale
+        step = lax.broadcasted_iota(jnp.int32, sn.shape, 0) % 4
+        new = lax.broadcasted_iota(jnp.int32, sn.shape, 1)
+        sn = jnp.where(low & (new // 4 == r) & (new % 4 <= step), sn, NEG)
+        o1, m1, l1 = pc[r, 0], pc[r, 1], pc[r, 2]
+        m = jnp.maximum(m1, jnp.maximum(rowmax(sp), rowmax(sn)))
+        ep, en = jnp.exp(sp - m[:, :1]), jnp.exp(sn - m[:, :1])
+        a1 = jnp.exp(m1 - m)
+        o = a1 * o1 + dot(ep.astype(BF16), pkv[1]) + dot(en.astype(BF16), dkv[1])
+        l = a1 * l1 + rowsum(ep) + rowsum(en)
+        for half in range(2):
+            t = slice(half * 16, half * 16 + 16)
+            at = half * 64 + r * 16
+            pk[0, at : at + 16] = o[t]
+            pk[1, at : at + 16] = jnp.where(lane < 64, m[t], l[t])
 
     got(("xm", 1), 1, 0, ROWS[1])
     fwd(("yf", 1, 1), 1, 0, ROWS[1], YN)
@@ -213,14 +272,15 @@
     got(("xp", 0), 3, 0, ROWS[0])
     fwd(("yf", 3, 0), 3, 0, ROWS[0], YN)
     fwd(("xpf", 0), 3, 0, ROWS[0], XP)
-    l_wk.wait()
-    l_wv.wait()
     l_wq.wait()
-    l_pas.wait()
+    for j in range(8):
+        project_new_q(j)
+    dqb[...] = accdq[...].astype(BF16)
+    send("dq", dqb, dqo, CN)
+    got(("xp", 2), 3, 0, ROWS[2])
+    fwd(("xpf", 2), 3, 0, ROWS[2], XP)
     got(("y", 3), 0, 1, ROWS[3])
     fwd(("xmy", 3), 0, 1, ROWS[3], XM)
-    got(("xp", 2), 3, 0, ROWS[2])
-    fwd(("xpf", 2), 3, 0, ROWS[2], XP)
     fwd(("xpy", 3), 0, 1, ROWS[3], XP)
     got(("xm", 3), 1, 0, ROWS[3])
     fwd(("xmf", 3), 1, 0, ROWS[3], XM)
@@ -228,72 +288,71 @@
     own("xp", 3, XP)
     own("xm", 2, XM)
     share(0, 1, 1)
+    arrange_new()
+    decode_cache(0)
     got(("xp", 1), 3, 0, ROWS[1])
     fwd(("yf", 3, 1), 3, 0, ROWS[1], YN)
     share(3, 0, 0)
     got(("xm", 0), 1, 0, ROWS[0])
     fwd(("yf", 1, 0), 1, 0, ROWS[0], YN)
     share(1, 0, 0)
+    decode_cache(1)
+    l_wk.wait()
+    l_wv.wait()
+    l_pas.wait()
     recv("wk", kv_rows(0, other))
     recv("wv", kv_rows(1, other))
     push_wo(0)
-    project_new(0)
-    project_new(1)
+    got(("xpy", 2), 3, 1, ROWS[2])
+    fwd(("xpfy", 2), 3, 1, ROWS[2], XP)
     got(("xmf", 1), 2, 0, ROWS[1])
     fwd(("yf", 2, 1), 2, 0, ROWS[1], YN)
-    got(("xpy", 2), 3, 1, ROWS[2])
-    fwd(("xpfy", 2), 3, 1, ROWS[2], XP)
-    project_new(2)
-    project_new(3)
+    decode_cache(2)
     got(("xpf", 0), 2, 0, ROWS[0])
     fwd(("yf", 2, 0), 2, 0, ROWS[0], YN)
     share(2, 0, 0)
     push_wo(1)
+    decode_cache(3)
     got(("xmy", 3), 1, 1, ROWS[3])
     fwd(("xmfy", 3), 1, 1, ROWS[3], XM)
     got(("y", 0), 0, 1, ROWS[0])
     got(("y", 1), 0, 1, ROWS[1])
     share(0, 1, 0)
-    for j in range(4, 8):
-        project_new(j)
-    dqb[...] = accdq[...].astype(BF16)
-    send("dq", dqb, dqo, CN)
+    for j in range(8):
+        project_new_kv(j)
     for i in range(2):
         dkv[i] = accdkv[:, i * HD : (i + 1) * HD].astype(BF16)
-    shared(0, 0)
-    project_kv(0, 0)
-    project_q(0, 0)
+    project(0, 0)
     got(("xpf", 2), 2, 0, ROWS[2])
     got(("xmf", 3), 2, 0, ROWS[3])
     share(2, 0, 1)
     push_wo(2)
-    shared(0, 1)
-    project_kv(0, 1)
-    project_q(0, 1)
+    project(0, 1)
     got(("yf", 3, 0), 3, 1, ROWS[0])
     got(("yf", 1, 1), 1, 1, ROWS[1])
     got(("yf", 3, 1), 3, 1, ROWS[1])
     got(("yf", 1, 0), 1, 1, ROWS[0])
     share(3, 1, 0)
     share(1, 1, 0)
-    shared(2, 0)
-    project_kv(2, 0)
-    project_q(2, 0)
     got(("xpy", 3), 3, 1, ROWS[3])
     share(3, 1, 1)
+    project(2, 0)
     got(("xmy", 2), 1, 1, ROWS[2])
     share(1, 1, 1)
     got(("xp", 3), 3, 0, ROWS[3])
     share(3, 0, 1)
     got(("xm", 2), 1, 0, ROWS[2])
     share(1, 0, 1)
+    project(3, 1)
     got(("xpfy", 2), 2, 1, ROWS[2])
     got(("xmfy", 3), 2, 1, ROWS[3])
     share(2, 1, 1)
     got(("yf", 2, 1), 2, 1, ROWS[1])
     got(("yf", 2, 0), 2, 1, ROWS[0])
     share(2, 1, 0)
-    for place in ((3, 1), (1, 1), (3, 0), (1, 0), (2, 1)):
+    project(1, 1)
+    last = ((3, 0), (1, 0), (2, 1))
+    for place in last:
         shared(*place)
         project_kv(*place)
 
@@ -303,7 +362,7 @@
     send("swapv", kv.at[1], kvprev.at[1], swap_dev)
     for i in range(3, WO_PIECES):
         push_wo(i)
-    for place in ((3, 1), (1, 1), (3, 0), (1, 0), (2, 1)):
+    for place in last:
         project_q(*place)
     qb[...] = accq[...].astype(BF16)
 
@@ -312,11 +371,7 @@
     mate_slot = lax.div(mate, 2)
 
     def gather_copy(d):
-        first = lax.div(s, 4) * 4
-        if d == 4:
-            to = mate
-        else:
-            to = first + lax.rem(s + d % 4, 4)
+        to = mate if d == 4 else along_z[d % 4]
         if d < 5:
             src, at = kv, slot
         else:
@@ -349,61 +404,15 @@
         e1 = jnp.exp(s1 - m1)
         held.append((m1, rowsum(e1), dot(e1.astype(BF16), kv[1])))
 
-    recv("dq", dqo)
-    q_low = jnp.where(low, dqb[...].astype(F32), dqo[...].astype(F32)).astype(BF16)
-    q_high = jnp.where(low, dqo[...].astype(F32), dqb[...].astype(F32)).astype(BF16)
-    q_all = jnp.concatenate(
-        [t[:, i * HD : (i + 1) * HD] for t in (q_low, q_high) for i in range(4)], axis=0
-    )
-    to = lax.broadcasted_iota(jnp.int32, (128, 128), 0)
-    frm = lax.broadcasted_iota(jnp.int32, (128, 128), 1)
-    source = (to // 64) * 64 + ((to % 16) // 4) * 16 + ((to % 64) // 16) * 4 + to % 4
-    q_rows = dot((source == frm).astype(BF16), q_all).astype(BF16)
-    l_ck.wait()
-    l_cv.wait()
-
-    def new_q(r):
-        return jnp.concatenate(
-            [q_rows[r * 16 : r * 16 + 16], q_rows[64 + r * 16 : 80 + r * 16]], axis=0
-        )
-
-    def decode_cache(r):
-        q = new_q(r)
-        sc = dot_t(q, ck[r, 0]) * scale
-        place = c * 2048 + lax.broadcasted_iota(jnp.int32, sc.shape, 1)
-        sc = jnp.where(place < len_ref[r], sc, NEG)
-        sn = dot_t(q, dkv[0]) * scale
-        step = lax.broadcasted_iota(jnp.int32, sn.shape, 0) % 4
-        new = lax.broadcasted_iota(jnp.int32, sn.shape, 1)
-        sn = jnp.where(low & (new // 4 == r) & (new % 4 <= step), sn, NEG)
-        m = jnp.maximum(rowmax(sc), rowmax(sn))
-        ec, en = jnp.exp(sc - m), jnp.exp(sn - m)
-        pc[r, 0] = dot(ec.astype(BF16), cv[r, 0]) + dot(en.astype(BF16), dkv[1])
-        pc[r, 1] = jnp.broadcast_to(m, (32, HD))
-        pc[r, 2] = jnp.broadcast_to(rowsum(ec) + rowsum(en), (32, HD))
-
-    def decode_passage(r):
-        q = new_q(r)
-        pkv = kvall[asg_ref[r]]
-        sp = dot_t(q, pkv[0]) * scale
-        o1, m1, l1 = pc[r, 0], pc[r, 1], pc[r, 2]
-        m = jnp.maximum(m1, rowmax(sp))
-        ep = jnp.exp(sp - m[:, :1])
-        a1 = jnp.exp(m1 - m)
-        o = a1 * o1 + dot(ep.astype(BF16), pkv[1])
-        l = a1 * l1 + rowsum(ep)
-        for half in range(2):
-            t = slice(half * 16, half * 16 + 16)
-            pk[half, 0, r * 16 : r * 16 + 16] = o[t]
-            pk[half, 1, r * 16 : r * 16 + 16] = m[t]
-            pk[half, 2, r * 16 : r * 16 + 16] = l[t]
-
-    for r in range(4):
-        decode_cache(r)
+    @pl.when(mine_parity)
+    def _():
+        gather_wait(mate_slot)
+        for d in range(5, 8):
+            gather_copy(d).start()
 
     second = lax.rem(s, 2) == 1
     recv("swapk", kvprev.at[0])
-    recv("swapv", kvprev.at[1])
+    scored = []
     for i in range(4):
         m1, l1, o1 = held[i]
         q = qb[:, i * HD : (i + 1) * HD]
@@ -411,20 +420,20 @@
         m = jnp.maximum(m1, rowmax(s0))
         a1 = jnp.exp(m1 - m)
         e0 = jnp.exp(s0 - m)
-        l = a1 * l1 + rowsum(e0)
-        o = (a1 * o1 + dot(e0.astype(BF16), kvprev[1])) / l
+        inv = 1.0 / (a1 * l1 + rowsum(e0))
+        scored.append((e0.astype(BF16), a1 * o1, inv))
+    recv("swapv", kvprev.at[1])
+    for i in range(4):
+        e0, o1, inv = scored[i]
+        o = (o1 + dot(e0, kvprev[1])) * inv
         ctx[c, :, i * HD : (i + 1) * HD] = o.astype(BF16)
         ref = ctx.at[c, :, pl.ds(i * HD, HD)]
         send(("ctx", i), ref, ref, CN)
 
-    @pl.when(mine_parity)
-    def _():
-        gather_wait(mate_slot)
-        for d in range(5, 8):
-            gather_copy(d).start()
-
     far = 1 - yl
     FLOW = (1, 3, 1, 3) * 2
+    base = pl.multiple_of(c * 4096, 4096)
+    far_base = pl.multiple_of(other * 4096, 4096)
 
     def width(ci):
         return WA if ci < 4 else WB
@@ -433,17 +442,26 @@
         at = ci * WA if ci < 4 else 4 * WA + (ci - 4) * WB
         return slice(at, at + width(ci))
 
+    def rows_of(core):
+        return pl.ds(pl.multiple_of(core * 16, 16), 16)
+
     def along(f):
         return (XP, XM) if f == 1 else (XM, XP)
 
+    def y_first(ci):
+        recv(("ry", ci), ray.at[ci])
+        parta[ci, yl] = (parta[ci, yl].astype(F32) + ray[ci].astype(F32)).astype(BF16)
+        for dx in (2, 1, 3, 0):
+            for q in range(2):
+                if dx or q:
+                    src = parta.at[ci, yl, lax.rem(x + dx, 4), rows_of(lax.rem(c + q, 2))]
+                    send(("ax", ci, dx, q), src, rax.at[ci, c, dx], dev(dx, 0, q))
+
     def x_block(ci, d):
-        at = lax.rem(x + d, 4)
-        if ci < 4:
-            return parta.at[ci, yl, at]
-        return partb.at[ci - 4, :, at]
+        return partb.at[ci - 4, :, lax.rem(x + d, 4)]
 
     def x_land(ci, k):
-        return rax.at[ci, k] if ci < 4 else rbx.at[ci - 4, k]
+        return rbx.at[ci - 4, k]
 
     def x_first(ci):
         send(("m1", ci), x_block(ci, 2), x_land(ci, 0), along(FLOW[ci])[0])
@@ -459,35 +477,39 @@
         block[...] = (block[...].astype(F32) + x_land(ci, 0)[...].astype(F32)).astype(BF16)
         send(("m3", ci), block, x_land(ci, 2), along(f)[0])
 
-    def x_end(ci):
+    def y_last(ci):
         recv(("m2", ci), x_land(ci, 1))
         recv(("m3", ci), x_land(ci, 2))
-        return (
-            x_block(ci, 0)[...].astype(F32)
-            + x_land(ci, 1)[...].astype(F32)
-            + x_land(ci, 2)[...].astype(F32)
-        )
-
-    def y_first(ci):
-        recv(("ry", ci), ray.at[ci])
-        parta[ci, yl] = (parta[ci, yl].astype(F32) + ray[ci].astype(F32)).astype(BF16)
-        x_first(ci)
-        x_second(ci)
-
-    def y_last(ci):
-        land = rbx.at[ci - 4, 1]
-        land[...] = x_end(ci).astype(BF16)
-        send(("ry", ci), land.at[far], rby.at[ci - 4], YN)
+        land = x_land(ci, 1)
+        land[...] = (
+            x_block(ci, 0)[...].astype(F32) + land[...].astype(F32) + x_land(ci, 2)[...].astype(F32)
+        ).astype(BF16)
+        for q in range(2):
+            src = land.at[far, rows_of(lax.rem(c + q, 2))]
+            send(("by", ci, q), src, rby.at[ci - 4, c], dev(0, 1, q))
+        send(("bl", ci), land.at[yl, rows_of(other)], rbl.at[ci - 4], CN)
 
     def finish(ci):
+        at = columns(ci).start
         if ci < 4:
-            total, keep, theirs = x_end(ci), fina.at[ci], finra.at[ci]
+            for dx in range(4):
+                for q in range(2):
+                    if dx or q:
+                        recv(("ax", ci, dx, q), rax.at[ci, lax.rem(c + q, 2), dx])
+            near = parta[ci, yl, x, rows_of(c)].astype(F32)
+            for dx in range(1, 4):
+                near += rax[ci, c, dx].astype(F32)
+            away = rax[ci, other, 0].astype(F32)
+            for dx in range(1, 4):
+                away += rax[ci, other, dx].astype(F32)
         else:
-            recv(("ry", ci), rby.at[ci - 4])
-            total = rbx[ci - 4, 1, yl].astype(F32) + rby[ci - 4].astype(F32)
-            keep, theirs = finb.at[ci - 4], finrb.at[ci - 4]
-        keep[...] = total.astype(BF16)
-        send(("fin", ci), keep.at[pl.ds(pl.multiple_of(other * 16, 16), 16)], theirs, CN)
+            for q in range(2):
+                recv(("by", ci, q), rby.at[ci - 4, lax.rem(c + q, 2)])
+            recv(("bl", ci), rbl.at[ci - 4])
+            near = rbx[ci - 4, 1, yl, rows_of(c)].astype(F32) + rby[ci - 4, c].astype(F32)
+            away = rbl[ci - 4].astype(F32) + rby[ci - 4, other].astype(F32)
+        pout[:, pl.ds(base + at, width(ci))] = near.astype(BF16)
+        pout[:, pl.ds(far_base + at, width(ci))] = away.astype(BF16)
 
     def out_own(ci):
         return dot(ctx[c], wo[c, :, columns(ci)])
@@ -502,23 +524,22 @@
             x_first(ci)
 
     l_wo.wait()
-    begun = out_own(0)
+    begun = out_own(7)
+    begun_b = out_own(0)
     for i in range(WO_PIECES):
         recv(("wo", i), wo.at[other, pl.ds(i * wo_rows, wo_rows), :])
     for i in range(4):
         recv(("ctx", i), ctx.at[other, :, pl.ds(i * HD, HD)])
-    out_rest(0, begun)
-    for ci in (4, 5):
-        out_rest(ci, out_own(ci))
-    x_second(4)
+    out_rest(7, begun)
+    x_second(7)
+    out_rest(0, begun_b)
+    out_rest(6, out_own(6))
+    x_second(6)
+    out_rest(2, out_own(2))
+    out_rest(5, out_own(5))
     x_second(5)
-    for ci in (1, 6, 7):
-        out_rest(ci, out_own(ci))
-    x_second(6)
-    x_second(7)
-    for ci in (2, 3):
-        out_rest(ci, out_own(ci))
-
+    out_rest(4, out_own(4))
+    x_pass(7)
     for j in range(4):
         @pl.when((2 * j + c != s) & (2 * j + c != mate))
         def _():
@@ -526,13 +547,14 @@
 
     for r in range(4):
         decode_passage(r)
-    send("part", pk.at[other], pko, CN)
-    x_pass(4)
-    x_pass(5)
+    send("part", pk, pko, CN)
+    x_pass(6)
+    x_second(4)
+    out_rest(1, out_own(1))
     y_first(0)
     recv("part", pko)
-    o1, m1, l1 = pk[c, 0], pk[c, 1], pk[c, 2]
-    o2, m2, l2 = pko[0], pko[1], pko[2]
+    o1, m1, l1 = pk[0], pk[1, :, 0:1], pk[1, :, 64:65]
+    o2, m2, l2 = pko[0], pko[1, :, 0:1], pko[1, :, 64:65]
     mm = jnp.maximum(m1, m2)
     a1, a2 = jnp.exp(m1 - mm), jnp.exp(m2 - mm)
     dec_ctx = ((a1 * o1 + a2 * o2) / (a1 * l1 + a2 * l2)).astype(BF16)
@@ -540,63 +562,52 @@
     frm = lax.broadcasted_iota(jnp.int32, (16, 64), 1)
     for i in range(4):
         pick = ((to // 4) * 16 + i * 4 + to % 4 == frm).astype(BF16)
-        dctx[c, :, i * HD : (i + 1) * HD] = dot(pick, dec_ctx).astype(BF16)
-    send("dctx", dctx.at[c], dctx.at[c], CN)
-    y_first(1)
-    x_pass(6)
-    x_pass(7)
-    recv("dctx", dctx.at[other])
+        for half in range(2):
+            chosen = dot(pick, dec_ctx[half * 64 : half * 64 + 64])
+            dctx[half, :, i * HD : (i + 1) * HD] = chosen.astype(BF16)
     for j in range(8):
         cols = slice(j * 512, (j + 1) * 512)
         dpart[j] = (dot(dctx[0], wo[0, :, cols]) + dot(dctx[1], wo[1, :, cols])).astype(BF16)
-    for i in range(1, 8):
+    for i in (6, 2, 5, 7, 1, 3, 4):
         dx, dy = i % 4, i // 4
         send(("dr", i), dpart.at[chip_at(dx, dy)], dr.at[i], dev(dx, dy))
     y_first(2)
-    x_pass(0)
-    y_first(3)
-    x_pass(1)
-    y_last(4)
-    y_last(5)
+    out_rest(3, out_own(3))
+    x_pass(5)
+    x_pass(4)
+    y_last(6)
+    y_first(1)
     total = dpart[chip].astype(F32)
     for i in range(1, 8):
         recv(("dr", i), dr.at[i])
         total = total + dr[i].astype(F32)
     dfull[c, chip] = total.astype(BF16)
-    for i in range(1, 8):
+    for i in (6, 2, 5, 7, 1, 3, 4):
         dx, dy = i % 4, i // 4
         ref = dfull.at[c, chip]
         send(("db", i), ref, ref, dev(dx, dy))
-    y_last(6)
     y_last(7)
-    x_pass(2)
-    x_pass(3)
+    y_last(4)
+    y_first(3)
     finish(0)
-    finish(1)
+    y_last(5)
     for i in range(1, 8):
         dx, dy = i % 4, i // 4
         recv(("db", i), dfull.at[c, chip_at(4 - dx, dy)])
     send("dall", dfull.at[c], dfull.at[c], CN)
-    for ci in (4, 5, 6, 7, 2, 3):
-        finish(ci)
+    finish(6)
+    finish(2)
+    finish(1)
+    finish(7)
+    finish(4)
+    finish(3)
+    finish(5)
 
     recv("dall", dfull.at[other])
     for a in range(2):
         for j in range(8):
             at = a * 4096 + j * 512
             dout[:, :, at : at + 512] = dfull[a, j].astype(F32).reshape(4, 4, 512).astype(BF16)
-    base = pl.multiple_of(c * 4096, 4096)
-    far_base = pl.multiple_of(other * 4096, 4096)
-    mine = pl.ds(pl.multiple_of(c * 16, 16), 16)
-    for ci in (0, 1, 4, 5, 6, 7, 2, 3):
-        at = columns(ci).start
-        if ci < 4:
-            keep, theirs = fina.at[ci], finra.at[ci]
-        else:
-            keep, theirs = finb.at[ci - 4], finrb.at[ci - 4]
-        pout[:, pl.ds(base + at, width(ci))] = keep[mine, :]
-        recv(("fin", ci), theirs)
-        pout[:, pl.ds(far_base + at, width(ci))] = theirs[...]
 
     for cp in sent:
         cp.wait_send()
@@ -649,16 +660,14 @@
             V((4, 2, 4, 32, WA), BF16),
             V((4, 2, 4, 32, WB), BF16),
             V((4, 4, 32, WA), BF16),
-            V((4, 3, 32, WA), BF16),
+            V((4, 2, 4, 16, WA), BF16),
             V((4, 3, 2, 32, WB), BF16),
-            V((4, 32, WB), BF16),
-            V((4, 32, WA), BF16),
-            V((4, 32, WB), BF16),
-            V((4, 16, WA), BF16),
+            V((4, 2, 16, WB), BF16),
             V((4, 16, WB), BF16),
             V((4, 3, 32, HD), F32),
-            V((2, 3, 64, HD), F32),
-            V((3, 64, HD), F32),
+            V((2, 128, HD), F32),
+            V((2, 128, HD), F32),
+            V((128, HD), BF16),
             V((2, DEC, 512), BF16),
             V((8, DEC, 512), BF16),
             V((8, DEC, 512), BF16),

time: 67.9 us -> 63 us (0.928)
  Pallas kernels: 67.1 us -> 62.2 us
    pallas_call x1, Pallas kernels: 65.2 us -> 60.4 us  [local(): pl.pallas_call(kernel, out_shape=shapes, in_specs=[any_spec] * 8 + [smem]...]
where the time goes in v3:
time: 63 us; the launch traced here: 62.9 us
  Pallas kernels  62.2 us (99%)
  between operations  0.64 us (1%)
    pallas_call x1, Pallas kernels, local(): pl.pallas_call(kernel, out_shape=shapes, in_specs=[any_spec] * 8 + [smem]...  60.4 us
    pallas_call x1, Pallas kernels, local(): pl.pallas_call(hand_over, out_shape=shapes, in_specs=[vmem] * 2, out_spec...  1.84 us

profile of v3, /device:TPU:1, one launch (start us, length us, event | category | flops | bytes accessed | tf_op | source)
XLA Modules:
  0.0 62.9 jit_solution(4486056309905268864)
XLA Ops:
  0.6 60.4 %layer.1 = (bf16[16,8192]{1,0:T(8,128)(2,1)}, bf16[4,4,8192]{2,1,0:T(4,128)(2,1)}) custom-call(bf16[256,512]{1,0:T(8,128)(2,1)} %pas.1, bf16[8192,512]{1,0:T(8,128)(2,1)} %wq_any.1, bf16[64,8192]{1,0:T(8,128)(2,1)} %bitcast.2, bf16[64,8192]{1,0:T(8,128)(2,1)} %bitcast.3, bf16[512,8192]{1,0:T(8,128)(2,1)} %wo_any.1, bf16[4,4,8192]{2,1,0:T(4,128)(2,1)} %dec_any.1, ...), custom_call_target="tpu_custom_call" | custom-call | tf_op jit(solution)/shard_map/layer/pallas_call | solution.py:634
  61.0 1.8 %hand_over.1 = (bf16[16,8192]{1,0:T(8,128)(2,1)}, bf16[4,4,8192]{2,1,0:T(4,128)(2,1)}) custom-call(bf16[16,8192]{1,0:T(8,128)(2,1)} %get-tuple-element.4.p_in, bf16[4,4,8192]{2,1,0:T(4,128)(2,1)} %get-tuple-element.5.d_in), custom_call_target="tpu_custom_call" | custom-call | tf_op jit(solution)/shard_map/hand_over/pallas_call | solution.py:688

commit v4 on v3

--- a/solution.py
+++ b/solution.py
@@ -360,12 +360,6 @@
         kv[i] = acckv[:, i * HD : (i + 1) * HD].astype(BF16)
     send("swapk", kv.at[0], kvprev.at[0], swap_dev)
     send("swapv", kv.at[1], kvprev.at[1], swap_dev)
-    for i in range(3, WO_PIECES):
-        push_wo(i)
-    for place in last:
-        project_q(*place)
-    qb[...] = accq[...].astype(BF16)
-
     mine_parity = lax.rem(s, 2) == c
     slot = lax.div(s, 2)
     mate_slot = lax.div(mate, 2)
@@ -394,6 +388,12 @@
             gather_copy(d).start()
         kvall[slot] = kv[...]
 
+    for i in range(3, WO_PIECES):
+        push_wo(i)
+    for place in last:
+        project_q(*place)
+    qb[...] = accq[...].astype(BF16)
+
     row = lax.broadcasted_iota(jnp.int32, (TOK, TOK), 0)
     col = lax.broadcasted_iota(jnp.int32, (TOK, TOK), 1)
     held = []
@@ -403,12 +403,6 @@
         m1 = rowmax(s1)
         e1 = jnp.exp(s1 - m1)
         held.append((m1, rowsum(e1), dot(e1.astype(BF16), kv[1])))
-
-    @pl.when(mine_parity)
-    def _():
-        gather_wait(mate_slot)
-        for d in range(5, 8):
-            gather_copy(d).start()
 
     second = lax.rem(s, 2) == 1
     recv("swapk", kvprev.at[0])
@@ -429,6 +423,12 @@
         ctx[c, :, i * HD : (i + 1) * HD] = o.astype(BF16)
         ref = ctx.at[c, :, pl.ds(i * HD, HD)]
         send(("ctx", i), ref, ref, CN)
+
+    @pl.when(mine_parity)
+    def _():
+        gather_wait(mate_slot)
+        for d in range(5, 8):
+            gather_copy(d).start()
 
     far = 1 - yl
     FLOW = (1, 3, 1, 3) * 2

time: 63 us -> 61.4 us (0.975)
  Pallas kernels: 62.2 us -> 60.6 us
    pallas_call x1, Pallas kernels: 60.4 us -> 58.8 us  [local(): pl.pallas_call(kernel, out_shape=shapes, in_specs=[any_spec] * 8 + [smem]...]
where the time goes in v4:
time: 61.4 us; the launch traced here: 61.3 us
  Pallas kernels  60.6 us (99%)
  between operations  0.64 us (1%)
    pallas_call x1, Pallas kernels, local(): pl.pallas_call(kernel, out_shape=shapes, in_specs=[any_spec] * 8 + [smem]...  58.8 us
    pallas_call x1, Pallas kernels, local(): pl.pallas_call(hand_over, out_shape=shapes, in_specs=[vmem] * 2, out_spec...  1.84 us

profile of v4, /device:TPU:1, one launch (start us, length us, event | category | flops | bytes accessed | tf_op | source)
XLA Modules:
  0.0 61.3 jit_solution(14787310241427160337)
XLA Ops:
  0.6 58.8 %layer.1 = (bf16[16,8192]{1,0:T(8,128)(2,1)}, bf16[4,4,8192]{2,1,0:T(4,128)(2,1)}) custom-call(bf16[256,512]{1,0:T(8,128)(2,1)} %pas.1, bf16[8192,512]{1,0:T(8,128)(2,1)} %wq_any.1, bf16[64,8192]{1,0:T(8,128)(2,1)} %bitcast.2, bf16[64,8192]{1,0:T(8,128)(2,1)} %bitcast.3, bf16[512,8192]{1,0:T(8,128)(2,1)} %wo_any.1, bf16[4,4,8192]{2,1,0:T(4,128)(2,1)} %dec_any.1, ...), custom_call_target="tpu_custom_call" | custom-call | tf_op jit(solution)/shard_map/layer/pallas_call | solution.py:634
  59.5 1.8 %hand_over.1 = (bf16[16,8192]{1,0:T(8,128)(2,1)}, bf16[4,4,8192]{2,1,0:T(4,128)(2,1)}) custom-call(bf16[16,8192]{1,0:T(8,128)(2,1)} %get-tuple-element.4.p_in, bf16[4,4,8192]{2,1,0:T(4,128)(2,1)} %get-tuple-element.5.d_in), custom_call_target="tpu_custom_call" | custom-call | tf_op jit(solution)/shard_map/hand_over/pallas_call | solution.py:688

commit v5 on v4

--- a/solution.py
+++ b/solution.py
@@ -244,25 +244,35 @@
         pc[r, 1] = jnp.broadcast_to(m, (32, HD))
         pc[r, 2] = jnp.broadcast_to(rowsum(ec), (32, HD))
 
-    def decode_passage(r):
-        q = new_q(r)
-        pkv = kvall[asg_ref[r]]
-        sp = dot_t(q, pkv[0]) * scale
-        sn = dot_t(q, dkv[0]) * scale
-        step = lax.broadcasted_iota(jnp.int32, sn.shape, 0) % 4
-        new = lax.broadcasted_iota(jnp.int32, sn.shape, 1)
-        sn = jnp.where(low & (new // 4 == r) & (new % 4 <= step), sn, NEG)
-        o1, m1, l1 = pc[r, 0], pc[r, 1], pc[r, 2]
-        m = jnp.maximum(m1, jnp.maximum(rowmax(sp), rowmax(sn)))
-        ep, en = jnp.exp(sp - m[:, :1]), jnp.exp(sn - m[:, :1])
-        a1 = jnp.exp(m1 - m)
-        o = a1 * o1 + dot(ep.astype(BF16), pkv[1]) + dot(en.astype(BF16), dkv[1])
-        l = a1 * l1 + rowsum(ep) + rowsum(en)
-        for half in range(2):
-            t = slice(half * 16, half * 16 + 16)
-            at = half * 64 + r * 16
-            pk[0, at : at + 16] = o[t]
-            pk[1, at : at + 16] = jnp.where(lane < 64, m[t], l[t])
+    def decode_passage():
+        held = []
+        for r in range(4):
+            q = new_q(r)
+            pkv = kvall[asg_ref[r]]
+            sp = dot_t(q, pkv[0]) * scale
+            sn = dot_t(q, dkv[0]) * scale
+            step = lax.broadcasted_iota(jnp.int32, sn.shape, 0) % 4
+            new = lax.broadcasted_iota(jnp.int32, sn.shape, 1)
+            sn = jnp.where(low & (new // 4 == r) & (new % 4 <= step), sn, NEG)
+            held.append((sp, sn, pkv[1]))
+        for r in range(4):
+            sp, sn, values = held[r]
+            m1, l1 = pc[r, 1], pc[r, 2]
+            m = jnp.maximum(m1, jnp.maximum(rowmax(sp), rowmax(sn)))
+            ep, en = jnp.exp(sp - m[:, :1]), jnp.exp(sn - m[:, :1])
+            a1 = jnp.exp(m1 - m)
+            l = a1 * l1 + rowsum(ep) + rowsum(en)
+            held[r] = (ep.astype(BF16), en.astype(BF16), values, a1, m, l)
+        for r in range(4):
+            ep, en, values, a1, m, l = held[r]
+            held[r] = (a1 * pc[r, 0] + dot(ep, values) + dot(en, dkv[1]), m, l)
+        for r in range(4):
+            o, m, l = held[r]
+            for half in range(2):
+                t = slice(half * 16, half * 16 + 16)
+                at = half * 64 + r * 16
+                pk[0, at : at + 16] = o[t]
+                pk[1, at : at + 16] = jnp.where(lane < 64, m[t], l[t])
 
     got(("xm", 1), 1, 0, ROWS[1])
     fwd(("yf", 1, 1), 1, 0, ROWS[1], YN)
@@ -545,8 +555,7 @@
         def _():
             gather_wait(j)
 
-    for r in range(4):
-        decode_passage(r)
+    decode_passage()
     send("part", pk, pko, CN)
     x_pass(6)
     x_second(4)

time: 61.4 us -> 60.7 us (0.989)
  Pallas kernels: 60.6 us -> 59.9 us
    pallas_call x1, Pallas kernels: 58.8 us -> 58.1 us  [local(): pl.pallas_call(kernel, out_shape=shapes, in_specs=[any_spec] * 8 + [smem]...]
where the time goes in v5:
time: 60.7 us; the launch traced here: 60.5 us
  Pallas kernels  59.9 us (99%)
  between operations  0.64 us (1%)
    pallas_call x1, Pallas kernels, local(): pl.pallas_call(kernel, out_shape=shapes, in_specs=[any_spec] * 8 + [smem]...  58.1 us
    pallas_call x1, Pallas kernels, local(): pl.pallas_call(hand_over, out_shape=shapes, in_specs=[vmem] * 2, out_spec...  1.84 us

profile of v5, /device:TPU:1, one launch (start us, length us, event | category | flops | bytes accessed | tf_op | source)
XLA Modules:
  0.0 60.5 jit_solution(5223947602174891229)
XLA Ops:
  0.6 58.1 %layer.1 = (bf16[16,8192]{1,0:T(8,128)(2,1)}, bf16[4,4,8192]{2,1,0:T(4,128)(2,1)}) custom-call(bf16[256,512]{1,0:T(8,128)(2,1)} %pas.1, bf16[8192,512]{1,0:T(8,128)(2,1)} %wq_any.1, bf16[64,8192]{1,0:T(8,128)(2,1)} %bitcast.2, bf16[64,8192]{1,0:T(8,128)(2,1)} %bitcast.3, bf16[512,8192]{1,0:T(8,128)(2,1)} %wo_any.1, bf16[4,4,8192]{2,1,0:T(4,128)(2,1)} %dec_any.1, ...), custom_call_target="tpu_custom_call" | custom-call | tf_op jit(solution)/shard_map/layer/pallas_call | solution.py:643
  58.7 1.8 %hand_over.1 = (bf16[16,8192]{1,0:T(8,128)(2,1)}, bf16[4,4,8192]{2,1,0:T(4,128)(2,1)}) custom-call(bf16[16,8192]{1,0:T(8,128)(2,1)} %get-tuple-element.4.p_in, bf16[4,4,8192]{2,1,0:T(4,128)(2,1)} %get-tuple-element.5.d_in), custom_call_target="tpu_custom_call" | custom-call | tf_op jit(solution)/shard_map/hand_over/pallas_call | solution.py:697
